TPU v7x, 512 devices: a whole 4x8x8 slice. The times are simulated.
512 devices in a mesh: context: 64 (over z_hi, y, core), tensor: 8 (over z_lo, x).
Axes of the slice: x: 4, y: 8, z: 8 (z_hi: 4, z_lo: 2; z = z_hi * 2 + z_lo), core: 2. Of those that a mesh axis runs over, the one named last changes fastest.
Arguments:
- query_slab: bfloat16 [4096, 8192], P('tensor', 'context'), may hold values from -6 to 6
- key_slab: bfloat16 [4096, 8192], P('tensor', 'context'), may hold values from -6 to 6
- value_slab: bfloat16 [4096, 8192], P('tensor', 'context'), may hold values from -6 to 6
- cotangent: bfloat16 [4096, 8192], P('tensor', 'context'), may hold values from -6 to 6
- filters: bfloat16 [256, 8192], P('tensor', 'context'), may hold values from -2 to 2
- skip_gain: float32 [4096], P('tensor'), may hold values from -1 to 1
Outputs:
- mixed: bfloat16 [4096, 8192], P('tensor', 'context')
- grad_query: bfloat16 [4096, 8192], P('tensor', 'context')
- grad_key: bfloat16 [4096, 8192], P('tensor', 'context')
- grad_value: bfloat16 [4096, 8192], P('tensor', 'context')
- filter_grad: float32 [256, 8192], P('tensor', 'context')
All inputs are finite; a program needn't handle non-finite values.
Results may differ from a plain program's by a relative error of at most 0.0095.
Values may be sent and summed in bfloat16 or wider, within the bound.
A program may use at most 64 MiB of HBM per device.

v0:
```python
import math

import jax
import jax.numpy as jnp
from jax import lax
from jax.sharding import PartitionSpec as P

HIGHEST = lax.Precision.HIGHEST


def make_tables(half_rows):
    full_rows = 2 * half_rows
    period = full_rows * 128
    row_index = jnp.arange(full_rows, dtype=jnp.int32)
    half_index = jnp.arange(half_rows, dtype=jnp.int32)
    col_index = jnp.arange(128, dtype=jnp.int32)
    first_angle = (row_index[:, None] * half_index[None, :] % full_rows).astype(jnp.float32) * (
        2.0 * math.pi / full_rows
    )
    first_table = jnp.concatenate([jnp.cos(first_angle), -jnp.sin(first_angle)], axis=0)
    twist_angle = (row_index[:, None] * col_index[None, :] % period).astype(jnp.float32) * (
        2.0 * math.pi / period
    )
    second_angle = (col_index[:, None] * col_index[None, :] % 128).astype(jnp.float32) * (
        2.0 * math.pi / 128
    )
    cosine = jnp.cos(second_angle)
    sine = jnp.sin(second_angle)
    forward_table = jnp.concatenate(
        [jnp.concatenate([cosine, -sine], 1), jnp.concatenate([sine, cosine], 1)], 0
    )
    inverse_table = jnp.concatenate(
        [jnp.concatenate([cosine, sine], 1), jnp.concatenate([-sine, cosine], 1)], 0
    )
    return (first_table, jnp.cos(twist_angle), jnp.sin(twist_angle), forward_table, inverse_table)


def transform(signal, tables):
    first_table, twist_cos, twist_sin, forward_table, inverse_table = tables
    full_rows = twist_cos.shape[0]
    section_one = jnp.einsum("km,bmn->bkn", first_table, signal, precision=HIGHEST)
    real_part = section_one[:, :full_rows]
    imag_part = section_one[:, full_rows:]
    turned = jnp.concatenate(
        [
            real_part * twist_cos + imag_part * twist_sin,
            imag_part * twist_cos - real_part * twist_sin,
        ],
        axis=2,
    )
    return jnp.einsum("bkn,nm->bkm", turned, forward_table, precision=HIGHEST)


def untransform(spectrum, tables):
    first_table, twist_cos, twist_sin, forward_table, inverse_table = tables
    period = twist_cos.shape[0] * 128
    section_two = jnp.einsum("bkn,nm->bkm", spectrum, inverse_table, precision=HIGHEST)
    real_part = section_two[..., :128]
    imag_part = section_two[..., 128:]
    turned = jnp.concatenate(
        [
            real_part * twist_cos - imag_part * twist_sin,
            real_part * twist_sin + imag_part * twist_cos,
        ],
        axis=1,
    )
    return jnp.einsum("km,bkn->bmn", first_table, turned, precision=HIGHEST) / period


def complex_product(left, right, conjugate):
    left_real = left[..., :128]
    left_imag = left[..., 128:]
    right_real = right[..., :128]
    right_imag = right[..., 128:]
    if conjugate:
        right_imag = -right_imag
    return jnp.concatenate(
        [
            left_real * right_real - left_imag * right_imag,
            left_real * right_imag + left_imag * right_real,
        ],
        axis=-1,
    )


def per_device(query_slab, key_slab, value_slab, cotangent, filters, skip_gain):
    contexts = lax.axis_size("context")
    local_channels, tokens_dev = query_slab.shape
    per_owner = local_channels // contexts
    length = tokens_dev * contexts
    half_rows = length // 128
    tables = make_tables(half_rows)
    place = lax.axis_index("context")
    product = (key_slab.astype(jnp.float32) * value_slab.astype(jnp.float32)).astype(jnp.bfloat16)
    grad_mix = (cotangent.astype(jnp.float32) * query_slab.astype(jnp.float32)).astype(jnp.bfloat16)
    whole_rows = lax.all_gather(filters, "context", axis=1, tiled=True)
    filter_row = lax.dynamic_index_in_dim(whole_rows, place // 2, 0, keepdims=False)
    filter_spec = transform(filter_row.astype(jnp.float32).reshape(1, half_rows, 128), tables)
    sent_product = product.reshape(contexts, per_owner, tokens_dev)
    sent_grad = grad_mix.reshape(contexts, per_owner, tokens_dev)
    own_product = lax.all_to_all(sent_product, "context", split_axis=0, concat_axis=2, tiled=True)
    own_grad = lax.all_to_all(sent_grad, "context", split_axis=0, concat_axis=2, tiled=True)
    count = own_product.shape[1]
    spec_prod = transform(own_product.astype(jnp.float32).reshape(count, half_rows, 128), tables)
    spec_grad = transform(own_grad.astype(jnp.float32).reshape(count, half_rows, 128), tables)
    conv_out = untransform(complex_product(spec_prod, filter_spec, False), tables)
    corr_out = untransform(complex_product(spec_grad, filter_spec, True), tables)
    cross = complex_product(spec_grad, spec_prod, True)
    conv_out = conv_out.reshape(1, count, length).astype(jnp.bfloat16)
    corr_out = corr_out.reshape(1, count, length).astype(jnp.bfloat16)
    conv_part, corr_part, cross = (conv_out, corr_out, cross.reshape((1,) + cross.shape))
    conv_back, corr_back = (
        lax.all_to_all(conv_part, "context", split_axis=2, concat_axis=0, tiled=True),
        lax.all_to_all(corr_part, "context", split_axis=2, concat_axis=0, tiled=True),
    )
    conv_back = conv_back.reshape(local_channels, tokens_dev).astype(jnp.float32)
    corr_back = corr_back.reshape(local_channels, tokens_dev).astype(jnp.float32)
    gain_col = skip_gain[:, None]
    forward_sum = conv_back + gain_col * product.astype(jnp.float32)
    mixed = (query_slab.astype(jnp.float32) * forward_sum).astype(jnp.bfloat16)
    grad_query = (cotangent.astype(jnp.float32) * forward_sum).astype(jnp.bfloat16)
    back_sum = corr_back + gain_col * grad_mix.astype(jnp.float32)
    grad_key = (back_sum * value_slab.astype(jnp.float32)).astype(jnp.bfloat16)
    grad_value = (back_sum * key_slab.astype(jnp.float32)).astype(jnp.bfloat16)
    partial_grad = untransform(jnp.sum(cross, axis=1), tables).reshape(length)
    every_grad = lax.all_gather(
        partial_grad.reshape(1, length).astype(jnp.bfloat16), "context", axis=0, tiled=True
    ).astype(jnp.float32)
    paired = jnp.sum(every_grad.reshape(contexts // 2, 2, length), axis=1)
    own_grad = lax.dynamic_slice_in_dim(paired, place * tokens_dev, tokens_dev, 1)
    squared = lax.psum(jnp.sum(own_grad * own_grad), ("context", "tensor"))
    entry_count = own_grad.shape[0] * lax.axis_size("tensor") * length
    factor = jnp.minimum(1.0, math.sqrt(entry_count) / jnp.sqrt(squared + 1e-06))
    filter_grad = (own_grad * factor).astype(jnp.float32)
    return (mixed, grad_query, grad_key, grad_value, filter_grad)


def solution(mesh):
    in_specs = (
        P("tensor", "context"),
        P("tensor", "context"),
        P("tensor", "context"),
        P("tensor", "context"),
        P("tensor", "context"),
        P("tensor"),
    )
    out_specs = (
        P("tensor", "context"),
        P("tensor", "context"),
        P("tensor", "context"),
        P("tensor", "context"),
        P("tensor", "context"),
    )
    return jax.shard_map(
        per_device, mesh=mesh, in_specs=in_specs, out_specs=out_specs, check_vma=False
    )
```

profile of v0, /device:TPU:1, one launch (start us, length us, event | category | flops | bytes accessed | tf_op | source)
XLA Modules:
  0.0 438.7 jit_solution(13784935971468257002)
XLA Ops:
  7.2 1.7 fusion.103
  8.8 17.6 %all-to-all-start = ((bf16[64,8,128]{2,1,0:T(8,128)(2,1)}), bf16[64,8,128]{2,1,0:T(8,128)(2,1)S(1)}, u32[]{:S(2)}, u32[]{:S(2)}) async-start(bf16[64,8,128]{2,1,0:T(8,128)(2,1)} %fusion.103), calls=%async_computation | async-start | bytes 262144 | tf_op jit(solution)/shard_map/all_to_all | solution.py:101
  27.2 84.7 %all_gather.6 = bf16[32,8192]{1,0:T(8,128)(2,1)S(1)} all-gather(bf16[32,128]{1,0:T(8,128)(2,1)} %param.10), channel_id=1, replica_groups=mesh['context'=64,'tensor'=8] {'context'}, dimensions={1}, use_global_device_ids=true | all-gather | bytes 532480 | tf_op jit(solution)/shard_map/all_gather | solution.py:96
  113.3 1.7 fusion.102
  114.9 4.9 %all-to-all-start.2 = ((bf16[64,8,128]{2,1,0:T(8,128)(2,1)}), bf16[64,8,128]{2,1,0:T(8,128)(2,1)S(1)}, u32[]{:S(2)}, u32[]{:S(2)}) async-start(bf16[64,8,128]{2,1,0:T(8,128)(2,1)} %fusion.102), calls=%async_computation.2 | async-start | bytes 262144 | tf_op jit(solution)/shard_map/all_to_all | solution.py:102
  120.9 11.6 %all-to-all-done.2 = bf16[64,8,128]{2,1,0:T(8,128)(2,1)S(1)} async-done(((bf16[64,8,128]{2,1,0:T(8,128)(2,1)}), bf16[64,8,128]{2,1,0:T(8,128)(2,1)S(1)}, u32[]{:S(2)}, u32[]{:S(2)}) %all-to-all-start.2) | async-done | bytes 131104 | tf_op jit(solution)/shard_map/all_to_all | solution.py:102
  133.4 1.9 fusion.17
  135.3 1.9 fusion.6
  138.3 1.1 fusion.10
  139.4 1.1 fusion.21
  140.8 1.1 fusion.2
  142.0 6.7 %copy.49 = bf16[1,8,8192]{1,0,2:T(2,128)(2,1)} copy(bf16[1,8,8192]{2,1,0:T(8,128)(2,1)S(1)} %convert_element_type.228) | data formatting | bytes 262144 | tf_op jit(solution)/shard_map/convert_element_type | solution.py:110
  149.3 45.4 %reduce.7 = bf16[8192,8]{1,0:T(8,128)(2,1)S(1)} reduce(bf16[8192,1,8]{2,1,0:T(2,128)(2,1)} %bitcast.97, bf16[]{:T(256)} %broadcast.164), dimensions={1}, to_apply=%bitcast.92.reduce_sub_computation | reduce | bytes 262146
  194.7 2.9 reshape.208
  197.6 4.5 %all-to-all-start.3 = ((bf16[64,2,512]{2,1,0:T(2,128)(2,1)}), bf16[64,2,512]{2,1,0:T(2,128)(2,1)S(1)}, u32[]{:S(2)}, u32[]{:S(2)}) async-start(bf16[64,2,512]{2,1,0:T(2,128)(2,1)} %reshape.208), calls=%async_computation.3 | async-start | bytes 262144 | tf_op jit(solution)/shard_map/all_to_all | solution.py:114
  202.7 0.6 reshape.194
  203.3 1.1 fusion.3
  204.5 6.9 %copy.42 = bf16[1,8,8192]{1,0,2:T(2,128)(2,1)} copy(bf16[1,8,8192]{2,1,0:T(8,128)(2,1)S(1)} %convert_element_type.216) | data formatting | bytes 262144 | tf_op jit(solution)/shard_map/convert_element_type | solution.py:109
  211.5 45.2 %reduce.6 = bf16[8192,8]{1,0:T(8,128)(2,1)S(1)} reduce(bf16[8192,1,8]{2,1,0:T(2,128)(2,1)} %bitcast.98, bf16[]{:T(256)} %broadcast.164), dimensions={1}, to_apply=%bitcast.90.reduce_sub_computation | reduce | bytes 262146
  256.7 2.9 reshape.206
  259.6 13.2 %all-to-all-start.1 = ((bf16[64,2,512]{2,1,0:T(2,128)(2,1)}), bf16[64,2,512]{2,1,0:T(2,128)(2,1)S(1)}, u32[]{:S(2)}, u32[]{:S(2)}) async-start(bf16[64,2,512]{2,1,0:T(2,128)(2,1)} %reshape.206), calls=%async_computation.1 | async-start | bytes 262144 | tf_op jit(solution)/shard_map/all_to_all | solution.py:113
  272.8 8.7 %reshape.209 = bf16[8192,1,8]{2,1,0:T(2,128)(2,1)} reshape(bf16[64,2,512]{2,1,0:T(2,128)(2,1)S(1)} %all-to-all-done.3) | data formatting | bytes 262144
  281.6 8.5 %bitcast_convert_fusion = f32[1,8,8192]{1,0,2:T(1,128)} fusion(bf16[8192,1,8]{2,1,0:T(2,128)(2,1)} %reshape.209), kind=kLoop, calls=%fused_computation.160 | loop fusion | flops 65536 | bytes 393216 | tf_op jit(solution)/shard_map/convert_element_type | solution.py:117
  290.0 2.8 copy.50
  292.8 8.7 %reshape.207 = bf16[8192,1,8]{2,1,0:T(2,128)(2,1)} reshape(bf16[64,2,512]{2,1,0:T(2,128)(2,1)S(1)} %all-to-all-done.1) | data formatting | bytes 262144
  301.6 8.4 %bitcast_convert_fusion.1 = f32[1,8,8192]{1,0,2:T(1,128)} fusion(bf16[8192,1,8]{2,1,0:T(2,128)(2,1)} %reshape.207), kind=kLoop, calls=%fused_computation.161 | loop fusion | flops 65536 | bytes 393216 | tf_op jit(solution)/shard_map/convert_element_type | solution.py:116
  310.0 3.4 copy.43
  313.4 9.2 %convert_reduce_fusion = f32[64,8192]{1,0:T(8,128)} fusion(bf16[64,1,8192]{2,1,0:T(2,128)(2,1)} %all-gather.3.cloned.1.call-done), kind=kLoop, calls=%fused_computation | loop fusion | flops 524288 | bytes 3145728 | tf_op jit(solution)/shard_map/reshape | solution.py:129
  322.6 2.8 reshape.191
  325.5 2.6 reduce_sum.28
  328.7 2.1 fusion.32
  330.8 99.5 %psum.7 = f32[]{:T(128)} all-reduce(f32[]{:T(128)} %multiply_reduce_fusion), channel_id=1, replica_groups=mesh['context'=64,'tensor'=8] {'context','tensor'}, use_global_device_ids=true, to_apply=%region_3.4 | all-reduce | flops 1 | bytes 8 | tf_op jit(solution)/shard_map/psum | solution.py:131
  (36 shorter events, 7.8 us)
Async XLA Ops:
  8.8 106.1 %all-to-all-start = ((bf16[64,8,128]{2,1,0:T(8,128)(2,1)}), bf16[64,8,128]{2,1,0:T(8,128)(2,1)S(1)}, u32[]{:S(2)}, u32[]{:S(2)}) async-start(bf16[64,8,128]{2,1,0:T(8,128)(2,1)} %fusion.103), calls=%async_computation | async-start | bytes 262144 | tf_op jit(solution)/shard_map/all_to_all | solution.py:101
  114.9 17.6 %all-to-all-start.2 = ((bf16[64,8,128]{2,1,0:T(8,128)(2,1)}), bf16[64,8,128]{2,1,0:T(8,128)(2,1)S(1)}, u32[]{:S(2)}, u32[]{:S(2)}) async-start(bf16[64,8,128]{2,1,0:T(8,128)(2,1)} %fusion.102), calls=%async_computation.2 | async-start | bytes 262144 | tf_op jit(solution)/shard_map/all_to_all | solution.py:102
  197.6 62.0 %all-to-all-start.3 = ((bf16[64,2,512]{2,1,0:T(2,128)(2,1)}), bf16[64,2,512]{2,1,0:T(2,128)(2,1)S(1)}, u32[]{:S(2)}, u32[]{:S(2)}) async-start(bf16[64,2,512]{2,1,0:T(2,128)(2,1)} %reshape.208), calls=%async_computation.3 | async-start | bytes 262144 | tf_op jit(solution)/shard_map/all_to_all | solution.py:114
  202.1 111.4 %all-gather.3.cloned.1.call-start = ((), (), s32[]{:S(2)}) async-start(), calls=%async_computation.4 | async-start | bytes 2129920 | tf_op jit(solution)/shard_map/all_gather | solution.py:126
  259.6 33.2 %all-to-all-start.1 = ((bf16[64,2,512]{2,1,0:T(2,128)(2,1)}), bf16[64,2,512]{2,1,0:T(2,128)(2,1)S(1)}, u32[]{:S(2)}, u32[]{:S(2)}) async-start(bf16[64,2,512]{2,1,0:T(2,128)(2,1)} %reshape.206), calls=%async_computation.1 | async-start | bytes 262144 | tf_op jit(solution)/shard_map/all_to_all | solution.py:113
  322.6 6.0 %copy-start = (bf16[512,128]{1,0:T(8,128)(2,1)S(1)}, bf16[512,128]{1,0:T(8,128)(2,1)}, u32[]{:S(2)}) copy-start(bf16[512,128]{1,0:T(8,128)(2,1)} %param.9) | copy-start | bytes 393220
  322.6 6.0 %copy-start.1 = (f32[512]{0:T(512)S(1)}, f32[512]{0:T(512)}, u32[]{:S(2)}) copy-start(f32[512]{0:T(512)} %param.11) | copy-start | bytes 6148
Sparse Core Ops, SparseCore 0:
  206.8 86.3 all-gather.2
where the time goes:
time: 444 us; the launch traced here: 439 us
  blocking collectives  184 us (41%)
  other arithmetic  129 us (29%)
  local copies, waits for them, and re-layouts  47.6 us (11%)
  starting transfers between devices  40.2 us (9%)
  between operations  15.3 us (3%)
  waiting for transfers between devices  11.7 us (3%)
  matrix products  11 us (2%)
    psum x1, blocking collectives, per_device(): squared = lax.psum(jnp.sum(own_grad * own_grad), ('context', 'tensor'))  99.5 us
    unnamed x2, other arithmetic  90.6 us
    all_gather x1, blocking collectives, per_device(): whole_rows = lax.all_gather(filters, 'context', axis=1, tiled=True)  84.7 us
    unnamed x10, local copies, waits for them, and re-layouts  24.5 us
    all_to_all x1, starting transfers between devices, per_device(): lax.all_to_all(sent_product, 'context', split_axis=0, concat_axis=2, tile...  17.6 us
    all_to_all x1, starting transfers between devices, per_device(): lax.all_to_all(conv_part, 'context', split_axis=2, concat_axis=0, tiled=T...  13.2 us
    all_to_all x1, waiting for transfers between devices, per_device(): lax.all_to_all(sent_grad, 'context', split_axis=0, concat_axis=2, tiled=T...  11.6 us
    reshape x1, other arithmetic, per_device(): paired = jnp.sum(every_grad.reshape(contexts // 2, 2, length), axis=1)  9.21 us
  transfers between devices with their start and end apart: 5, of which 1 were waited for; matrix products, arithmetic and copies ran while one was open for 23% of the time, Pallas kernels for 0%

commit v1 on v0

v1 whole, which is shorter than its diff:
```python
import functools
import math

import jax
import jax.numpy as jnp
from jax import lax
from jax.experimental import pallas as pl
from jax.experimental.pallas import tpu as pltpu
from jax.sharding import PartitionSpec as P

MESH = pl.DeviceIdType.MESH
F32 = jnp.float32
BF16 = jnp.bfloat16
LANES = 128
OWN = 8


def exchange(lanes=LANES):
    row = lax.broadcasted_iota(jnp.int32, (lanes, lanes), 0)
    col = lax.broadcasted_iota(jnp.int32, (lanes, lanes), 1)
    return (row + col == lanes - 1).astype(BF16)


def kernel(
    C, T, entries,
    q_hbm, k_hbm, v_hbm, c_hbm, f_hbm, gain_hbm,
    mixed_ref, gq_ref, gk_ref, gv_ref, fg_ref,
    q_ref, k_ref, v_ref, c_ref, f_ref, gain_ref,
    gain_col, fsend, frecv, msend, mrecv, toep, z2, acc, gcat, bsend, brecv,
    raw, raw_other, gsend, grecv, tsend, trecv,
    load_sem, send_sem, recv_sem,
):
    me = lax.axis_index("context")
    ten = lax.axis_index("tensor")
    half = C // 2
    pair = me // 2
    core = me % 2
    rows = C * OWN

    loads = [
        pltpu.make_async_copy(src, dst, load_sem.at[n])
        for n, (src, dst) in enumerate(
            [(f_hbm, f_ref), (k_hbm, k_ref), (v_hbm, v_ref), (q_hbm, q_ref), (c_hbm, c_ref), (gain_hbm, gain_ref)]
        )
    ]
    for load in loads:
        load.start()

    def context_peer(k):
        return lax.rem(me + k, C)

    barrier = pltpu.get_barrier_semaphore()

    def greet(k, _):
        pl.semaphore_signal(barrier, inc=1, device_id=(context_peer(k), ten), device_id_type=MESH)
        return 0

    lax.fori_loop(1, C, greet, 0)
    for k in range(1, T):
        pl.semaphore_signal(barrier, inc=1, device_id=(me, lax.rem(ten + k, T)), device_id_type=MESH)

    flip = exchange()

    loads[0].wait()
    taps = jnp.dot(f_ref[...], flip, preferred_element_type=F32)
    for r in range(half):
        fsend[r] = taps[r : r + 1]

    for load in loads[1:5]:
        load.wait()
    product = (k_ref[...].astype(F32) * v_ref[...].astype(F32)).astype(BF16)
    mirrored = jnp.dot(product, flip, preferred_element_type=F32).reshape(C, OWN, LANES)
    gmix = (q_ref[...].astype(F32) * c_ref[...].astype(F32)).reshape(C, OWN, LANES)
    msend[...] = jnp.concatenate([mirrored, gmix], axis=1).astype(BF16)

    pl.semaphore_wait(barrier, C - 1 + T - 1)

    def send(src, dst, phase, peer):
        return pltpu.make_async_remote_copy(
            src_ref=src, dst_ref=dst, send_sem=send_sem.at[phase], recv_sem=recv_sem.at[phase],
            device_id=peer, device_id_type=MESH,
        )

    def send_taps(k, _):
        to = context_peer(k)
        send(fsend.at[to // 2], frecv.at[me], 0, (to, ten)).start()
        return 0

    def send_main(k, _):
        to = context_peer(k)
        send(msend.at[to], mrecv.at[me], 1, (to, ten)).start()
        return 0

    lax.fori_loop(1, C, send_taps, 0)
    lax.fori_loop(1, C, send_main, 0)

    frecv[me] = fsend[pair]
    mrecv[me] = msend[me]
    loads[5].wait()
    for n in range(gain_ref.shape[0]):
        wide = jnp.broadcast_to(gain_ref[n : n + 1, :], (LANES, LANES))
        gain_col[n * LANES : (n + 1) * LANES, :] = wide.T
    toep[0] = jnp.zeros((LANES, LANES), BF16)
    z2[half * 16 :, :] = jnp.zeros((z2.shape[0] - half * 16, 2 * LANES), BF16)
    gcat[rows:, :] = jnp.zeros((gcat.shape[0] - rows, 2 * LANES), BF16)

    send(frecv.at[pl.ds(0, C - 1)], frecv.at[pl.ds(0, C - 1)], 0, (me, ten)).wait_recv()
    row = lax.broadcasted_iota(jnp.int32, (LANES, LANES), 0)
    col = lax.broadcasted_iota(jnp.int32, (LANES, LANES), 1)
    lower = col <= row

    def build(d, last):
        wide = jnp.broadcast_to(frecv[d], (LANES, LANES))
        turned = pltpu.roll(wide, 1, 1, stride=1, stride_axis=0)
        toep[d + 1] = jnp.where(lower, turned, last).astype(BF16)
        return turned

    lax.fori_loop(0, C, build, jnp.zeros((LANES, LANES), F32))

    send(mrecv.at[pl.ds(0, C - 1)], mrecv.at[pl.ds(0, C - 1)], 1, (me, ten)).wait_recv()
    zero = jnp.zeros((OWN, LANES), F32)
    for j in range(half):
        two = []
        for i in (2 * j, 2 * j + 1):
            two.append(jnp.concatenate([mrecv[C - 1 - i].astype(F32)[:OWN], mrecv[i].astype(F32)[OWN:]], axis=0))
        z2[16 * j : 16 * j + 16, :] = jnp.concatenate(two, axis=1).astype(BF16)

    def weight(d):
        top = jnp.concatenate([toep[2 * d + 1], toep[2 * d]], axis=1)
        low = jnp.concatenate([toep[2 * d + 2], toep[2 * d + 1]], axis=1)
        return jnp.concatenate([top, low], axis=0)

    step = min(4, half)
    for d0 in range(0, half, step):
        size = 16 * (half - d0)
        left = jnp.concatenate([z2[16 * (d0 + u) : 16 * (d0 + u) + size, :] for u in range(step)], axis=1)
        right = jnp.concatenate([weight(d0 + u) for u in range(step)], axis=0)
        part = jnp.dot(left, right, preferred_element_type=F32)
        if d0 == 0:
            acc[...] = part
        else:
            acc[0:size, :] += part

    for i in range(C):
        m = C - 1 - i
        conv = acc[16 * (m // 2) : 16 * (m // 2) + OWN, (m % 2) * LANES : (m % 2 + 1) * LANES]
        corr = acc[16 * (i // 2) + OWN : 16 * (i // 2) + 16, (i % 2) * LANES : (i % 2 + 1) * LANES]
        bsend[i] = jnp.concatenate([conv, corr], axis=0).astype(BF16)

    def send_back(k, _):
        to = context_peer(k)
        send(bsend.at[to], brecv.at[me], 2, (to, ten)).start()
        return 0

    lax.fori_loop(1, C, send_back, 0)
    brecv[me] = bsend[me]

    whole = mrecv[...].astype(F32)
    xt = whole[:, :OWN].reshape(rows, LANES).T.astype(BF16)
    gpart = whole[:, OWN:]
    after = jnp.concatenate([gpart[1:], zero[None]], axis=0)
    gcat[0:rows, :] = jnp.concatenate([gpart, after], axis=2).reshape(rows, 2 * LANES).astype(BF16)

    def lags(e, depth):
        first = pl.multiple_of(16 * e, 16)
        return jnp.dot(xt[:, :depth], gcat[pl.ds(first, depth), :], preferred_element_type=F32)

    def skew(block):
        return pltpu.roll(block, 1, 1, stride=1, stride_axis=0)

    def gather(depth, group):
        def body(n, last):
            parts = [lags(group * n + u, depth) for u in range(group)]
            for u in reversed(range(group)):
                for side in (1, 0):
                    turned = skew(parts[u][:, side * LANES : (side + 1) * LANES])
                    place = 2 * (group * n + u) + side
                    raw[place] = jnp.sum(jnp.where(lower, turned, last), axis=0, keepdims=True)
                    last = turned
            return last

        return body

    group = min(4, half // 2)
    quarter = half // 2 // group
    last = jnp.zeros((LANES, LANES), F32)
    late = gather(rows // 2, group)
    early = gather(rows, group)
    last = lax.fori_loop(0, quarter, lambda n, s: late(2 * quarter - 1 - n, s), last)
    last = lax.fori_loop(0, quarter, lambda n, s: early(quarter - 1 - n, s), last)

    other = me + 1 - 2 * core
    swap = send(raw, raw_other, 3, (other, ten))
    swap.start()
    swap.wait_recv()
    total = raw[...] + raw_other[...]
    size2 = jnp.sum(jnp.sum(total * total, axis=0), axis=1, keepdims=True)
    size_row = jnp.broadcast_to(size2, (1, LANES))
    for i in range(C):
        gsend[i] = jnp.concatenate([total[i], size_row], axis=0)

    base = half * core
    offset = lax.rem(me, half)
    mine = core == me // half

    def send_grad(k, _):
        to = base + lax.rem(offset + k, half)
        send(gsend.at[to], grecv.at[pair], 4, (to, ten)).start()
        return 0

    lax.fori_loop(1, half, send_grad, 0)
    straight = base + offset

    @pl.when(mine)
    def _():
        grecv[pair] = gsend[me]

    @pl.when(jnp.logical_not(mine))
    def _():
        send(gsend.at[straight], grecv.at[pair], 4, (straight, ten)).start()

    def grads(count):
        part = pl.ds(0, count)
        return send(gsend.at[part], grecv.at[part], 4, (me, ten))

    @pl.when(mine)
    def _():
        grads(half - 1).wait_recv()

    @pl.when(jnp.logical_not(mine))
    def _():
        grads(half).wait_recv()

    square = jnp.sum(grecv[:, 1:2, :], axis=0)
    tsend[...] = square
    trecv[ten] = square
    for k in range(1, T):
        send(tsend, trecv.at[ten], 5, (me, lax.rem(ten + k, T))).start()

    send(brecv.at[pl.ds(0, C - 1)], brecv.at[pl.ds(0, C - 1)], 2, (me, ten)).wait_recv()
    back = brecv[...].astype(F32)
    conv = jnp.dot(back[:, :OWN].reshape(rows, LANES).astype(BF16), flip, preferred_element_type=F32)
    corr = back[:, OWN:].reshape(rows, LANES)
    gain = gain_col[...]
    kf = k_ref[...].astype(F32)
    vf = v_ref[...].astype(F32)
    forward = conv + gain * (kf * vf).astype(BF16).astype(F32)
    qf = q_ref[...].astype(F32)
    cf = c_ref[...].astype(F32)
    mixed_ref[...] = (qf * forward).astype(BF16)
    gq_ref[...] = (cf * forward).astype(BF16)
    backward = corr + gain * (qf * cf).astype(BF16).astype(F32)
    gk_ref[...] = (backward * vf).astype(BF16)
    gv_ref[...] = (backward * kf).astype(BF16)

    if T > 1:
        part = pl.ds(0, T - 1)
        send(trecv.at[part], trecv.at[part], 5, (me, ten)).wait_recv()
    squared = jnp.sum(trecv[...], axis=0)
    factor = jnp.minimum(1.0, math.sqrt(entries) / jnp.sqrt(squared + 1e-6))
    for r in range(half):
        fg_ref[r : r + 1, :] = grecv[r, 0:1, :] * factor

    send(frecv.at[pl.ds(0, C - 1)], frecv.at[pl.ds(0, C - 1)], 0, (me, ten)).wait_send()
    send(msend.at[pl.ds(0, C - 1)], msend.at[pl.ds(0, C - 1)], 1, (me, ten)).wait_send()
    send(bsend.at[pl.ds(0, C - 1)], bsend.at[pl.ds(0, C - 1)], 2, (me, ten)).wait_send()
    swap.wait_send()

    @pl.when(mine)
    def _():
        grads(half - 1).wait_send()

    @pl.when(jnp.logical_not(mine))
    def _():
        grads(half).wait_send()

    if T > 1:
        part = pl.ds(0, T - 1)
        send(trecv.at[part], trecv.at[part], 5, (me, ten)).wait_send()


def per_device(C, T, query_slab, key_slab, value_slab, cotangent, filters, skip_gain):
    channels, tokens = query_slab.shape
    half = C // 2
    rows = C * OWN
    entries = half * T * tokens * C
    slab = jax.ShapeDtypeStruct((channels, tokens), BF16)
    gains = skip_gain.reshape(channels // LANES, LANES)
    any_spec = pl.BlockSpec(memory_space=pl.ANY)
    vmem_spec = pl.BlockSpec(memory_space=pltpu.VMEM)
    return pl.pallas_call(
        functools.partial(kernel, C, T, entries),
        out_shape=(slab, slab, slab, slab, jax.ShapeDtypeStruct((half, tokens), F32)),
        in_specs=[any_spec] * 6,
        out_specs=(vmem_spec,) * 5,
        scratch_shapes=[
            pltpu.VMEM((channels, tokens), BF16),
            pltpu.VMEM((channels, tokens), BF16),
            pltpu.VMEM((channels, tokens), BF16),
            pltpu.VMEM((channels, tokens), BF16),
            pltpu.VMEM((half, tokens), BF16),
            pltpu.VMEM(gains.shape, F32),
            pltpu.VMEM((channels, LANES), F32),
            pltpu.VMEM((half, 1, LANES), F32),
            pltpu.VMEM((C, 1, LANES), F32),
            pltpu.VMEM((C, 16, LANES), BF16),
            pltpu.VMEM((C, 16, LANES), BF16),
            pltpu.VMEM((C + 1, LANES, LANES), BF16),
            pltpu.VMEM((16 * (half + 4), 2 * LANES), BF16),
            pltpu.VMEM((16 * half, 2 * LANES), F32),
            pltpu.VMEM((2 * rows, 2 * LANES), BF16),
            pltpu.VMEM((C, 16, LANES), BF16),
            pltpu.VMEM((C, 16, LANES), BF16),
            pltpu.VMEM((C, 1, LANES), F32),
            pltpu.VMEM((C, 1, LANES), F32),
            pltpu.VMEM((C, 2, LANES), F32),
            pltpu.VMEM((half, 2, LANES), F32),
            pltpu.VMEM((1, LANES), F32),
            pltpu.VMEM((T, 1, LANES), F32),
            pltpu.SemaphoreType.DMA((6,)),
            pltpu.SemaphoreType.DMA((6,)),
            pltpu.SemaphoreType.DMA((6,)),
        ],
        compiler_params=pltpu.CompilerParams(
            collective_id=0, has_side_effects=True, vmem_limit_bytes=40 * 1024 * 1024
        ),
        name="hyena",
    )(query_slab, key_slab, value_slab, cotangent, filters, gains)


def solution(mesh):
    C, T = mesh.shape["context"], mesh.shape["tensor"]
    slab = P("tensor", "context")
    return jax.shard_map(
        functools.partial(per_device, C, T),
        mesh=mesh,
        in_specs=(slab, slab, slab, slab, slab, P("tensor")),
        out_specs=(slab, slab, slab, slab, slab),
        check_vma=False,
    )
```

time: 444 us -> 57.9 us (0.13); the launches traced: 439 us -> 57.7 us
  blocking collectives: 184 us -> 0 us
  other arithmetic: 129 us -> 0 us
  Pallas kernels: 0 us -> 48.8 us
  starting transfers between devices: 40.2 us -> 0 us
  local copies, waits for them, and re-layouts: 47.6 us -> 8.21 us
  between operations: 15.3 us -> 0.66 us
  waiting for transfers between devices: 11.7 us -> 0 us
  matrix products: 11 us -> 0 us
    psum x1 -> x0, blocking collectives: 99.5 us -> none  [per_device(): squared = lax.psum(jnp.sum(own_grad * own_grad), ('context', 'tensor'))]
    unnamed x2 -> x0, other arithmetic: 90.6 us -> none
    all_gather x1 -> x0, blocking collectives: 84.7 us -> none  [per_device(): whole_rows = lax.all_gather(filters, 'context', axis=1, tiled=True)]
    pallas_call x0 -> x1, Pallas kernels: none -> 48.8 us  [per_device(): pl.pallas_call(functools.partial(kernel, C, T, entries), out_shape=(slab,...]
    all_to_all x4 -> x0, starting transfers between devices: 40.1 us -> none  [the longest x1 17.6 us: per_device(): lax.all_to_all(sent_product, 'context', split_axis=0, concat_axis=2, tile...]
    convert_element_type x6 -> x0, local copies, waits for them, and re-layouts: 20 us -> none  [the longest x2 7.01 us: per_device(): conv_out = conv_out.reshape(1, count, length).astype(jnp.bfloat16)]
    convert_element_type x3 -> x0, other arithmetic: 19 us -> none  [the longest x1 8.45 us: per_device(): corr_back.reshape(local_channels, tokens_dev).astype(jnp.float32)]
    unnamed x10 -> x17, local copies, waits for them, and re-layouts: 24.5 us -> 8.21 us
  transfers between devices with their start and end apart: 5 -> 0, of which waited for: 1 -> 0; matrix products, arithmetic and copies ran while one was open for 23% -> 0% of each run, Pallas kernels for 0% -> 0%
where the time goes in v1:
time: 57.9 us; the launch traced here: 57.7 us
  Pallas kernels  48.8 us (84%)
  local copies, waits for them, and re-layouts  8.21 us (14%)
  between operations  0.66 us (1%)
    pallas_call x1, Pallas kernels, per_device(): pl.pallas_call(functools.partial(kernel, C, T, entries), out_shape=(slab,...  48.8 us
    unnamed x17, local copies, waits for them, and re-layouts  8.21 us

profile of v1, /device:TPU:1, one launch (start us, length us, event | category | flops | bytes accessed | tf_op | source)
XLA Modules:
  0.0 57.7 jit_solution(6526030088353937863)
XLA Ops:
  0.6 0.0 copy-start
  0.6 0.9 %copy-done = bf16[512,128]{1,0:T(8,128)(2,1)S(1)} copy-done((bf16[512,128]{1,0:T(8,128)(2,1)S(1)}, bf16[512,128]{1,0:T(8,128)(2,1)}, u32[]{:S(2)}) %copy-start) | copy-done | bytes 131096
  1.5 0.0 copy-start.1
  1.5 0.9 %copy-done.1 = bf16[512,128]{1,0:T(8,128)(2,1)S(1)} copy-done((bf16[512,128]{1,0:T(8,128)(2,1)S(1)}, bf16[512,128]{1,0:T(8,128)(2,1)}, u32[]{:S(2)}) %copy-start.1) | copy-done | bytes 131096
  2.4 0.0 copy-start.2
  2.4 0.9 %copy-done.2 = bf16[512,128]{1,0:T(8,128)(2,1)S(1)} copy-done((bf16[512,128]{1,0:T(8,128)(2,1)S(1)}, bf16[512,128]{1,0:T(8,128)(2,1)}, u32[]{:S(2)}) %copy-start.2) | copy-done | bytes 131096
  3.3 0.0 copy-start.3
  3.4 0.9 %copy-done.3 = bf16[512,128]{1,0:T(8,128)(2,1)S(1)} copy-done((bf16[512,128]{1,0:T(8,128)(2,1)S(1)}, bf16[512,128]{1,0:T(8,128)(2,1)}, u32[]{:S(2)}) %copy-start.3) | copy-done | bytes 131096
  4.3 0.0 copy-start.4
  4.3 0.7 %copy-done.4 = bf16[32,128]{1,0:T(8,128)(2,1)S(1)} copy-done((bf16[32,128]{1,0:T(8,128)(2,1)S(1)}, bf16[32,128]{1,0:T(8,128)(2,1)}, u32[]{:S(2)}) %copy-start.4) | copy-done | bytes 8216
  5.0 0.0 copy-start.5
  5.0 0.7 %copy-done.5 = f32[512]{0:T(512)S(1)} copy-done((f32[512]{0:T(512)S(1)}, f32[512]{0:T(512)}, u32[]{:S(2)}) %copy-start.5) | copy-done | bytes 2072
  5.6 48.8 %hyena.1 = (bf16[512,128]{1,0:T(8,128)(2,1)S(1)}, bf16[512,128]{1,0:T(8,128)(2,1)S(1)}, bf16[512,128]{1,0:T(8,128)(2,1)S(1)}, bf16[512,128]{1,0:T(8,128)(2,1)S(1)}, f32[32,128]{1,0:T(8,128)S(1)}) custom-call(bf16[512,128]{1,0:T(8,128)(2,1)S(1)} %copy-done, bf16[512,128]{1,0:T(8,128)(2,1)S(1)} %copy-done.1, bf16[512,128]{1,0:T(8,128)(2,1)S(1)} %copy-done.2, ...), custom_call_target="tpu_custom_call" | custom-call | tf_op jit(solution)/shard_map/hyena/pallas_call | solution.py:291
  54.5 0.7 %copy.16 = bf16[512,128]{1,0:T(8,128)(2,1)} copy(bf16[512,128]{1,0:T(8,128)(2,1)S(1)} %get-tuple-element.10) | data formatting | bytes 262144
  55.1 0.7 %copy.17 = bf16[512,128]{1,0:T(8,128)(2,1)} copy(bf16[512,128]{1,0:T(8,128)(2,1)S(1)} %get-tuple-element.11) | data formatting | bytes 262144
  55.8 0.7 %copy.18 = bf16[512,128]{1,0:T(8,128)(2,1)} copy(bf16[512,128]{1,0:T(8,128)(2,1)S(1)} %get-tuple-element.12) | data formatting | bytes 262144
  56.4 0.7 %copy.19 = bf16[512,128]{1,0:T(8,128)(2,1)} copy(bf16[512,128]{1,0:T(8,128)(2,1)S(1)} %get-tuple-element.13) | data formatting | bytes 262144
  57.1 0.6 %copy.20 = f32[32,128]{1,0:T(8,128)} copy(f32[32,128]{1,0:T(8,128)S(1)} %get-tuple-element.14) | data formatting | bytes 32768
Async XLA Ops:
  0.6 0.9 %copy-start = (bf16[512,128]{1,0:T(8,128)(2,1)S(1)}, bf16[512,128]{1,0:T(8,128)(2,1)}, u32[]{:S(2)}) copy-start(bf16[512,128]{1,0:T(8,128)(2,1)} %q_hbm.1) | copy-start | bytes 393220
  1.5 0.9 %copy-start.1 = (bf16[512,128]{1,0:T(8,128)(2,1)S(1)}, bf16[512,128]{1,0:T(8,128)(2,1)}, u32[]{:S(2)}) copy-start(bf16[512,128]{1,0:T(8,128)(2,1)} %k_hbm.1) | copy-start | bytes 393220
  2.4 0.9 %copy-start.2 = (bf16[512,128]{1,0:T(8,128)(2,1)S(1)}, bf16[512,128]{1,0:T(8,128)(2,1)}, u32[]{:S(2)}) copy-start(bf16[512,128]{1,0:T(8,128)(2,1)} %v_hbm.1) | copy-start | bytes 393220
  3.3 0.9 %copy-start.3 = (bf16[512,128]{1,0:T(8,128)(2,1)S(1)}, bf16[512,128]{1,0:T(8,128)(2,1)}, u32[]{:S(2)}) copy-start(bf16[512,128]{1,0:T(8,128)(2,1)} %c_hbm.1) | copy-start | bytes 393220
  4.3 0.7 %copy-start.4 = (bf16[32,128]{1,0:T(8,128)(2,1)S(1)}, bf16[32,128]{1,0:T(8,128)(2,1)}, u32[]{:S(2)}) copy-start(bf16[32,128]{1,0:T(8,128)(2,1)} %f_hbm.1) | copy-start | bytes 24580
  5.0 0.7 %copy-start.5 = (f32[512]{0:T(512)S(1)}, f32[512]{0:T(512)}, u32[]{:S(2)}) copy-start(f32[512]{0:T(512)} %param.11) | copy-start | bytes 6148

commit v2 on v1

v2 whole, which is shorter than its diff:
```python
import functools
import math

import jax
import jax.numpy as jnp
from jax import lax
from jax.experimental import pallas as pl
from jax.experimental.pallas import tpu as pltpu
from jax.sharding import PartitionSpec as P

MESH = pl.DeviceIdType.MESH
F32 = jnp.float32
BF16 = jnp.bfloat16
LANES = 128
VMEM_BYTES = 62 * 1024 * 1024
UNROLL = 8
OWN = 8


def exchange(lanes=LANES):
    row = lax.broadcasted_iota(jnp.int32, (lanes, lanes), 0)
    col = lax.broadcasted_iota(jnp.int32, (lanes, lanes), 1)
    return (row + col == lanes - 1).astype(BF16)


def far(i, n):
    return n // 2 + ((i + 1) // 2) * (1 - 2 * (i % 2))


def kernel(
    C, T,
    q_hbm, k_hbm, v_hbm, c_hbm, f_hbm,
    brecv, grads_out, trecv,
    q_ref, k_ref, v_ref, c_ref, f_ref,
    fsend, frecv, msend, mrecv, toep, z2, acc, gcat, bsend,
    raw, raw_other, gsend, grecv, tsend,
    load_sem, send_sem, recv_sem,
):
    me = lax.axis_index("context")
    ten = lax.axis_index("tensor")
    half = C // 2
    Z = max(1, C // 16)
    Y = half // Z
    pair = me // 2
    core = me % 2
    rows = C * OWN

    loads = [
        pltpu.make_async_copy(src, dst, load_sem.at[n])
        for n, (src, dst) in enumerate(
            [(f_hbm, f_ref), (k_hbm, k_ref), (v_hbm, v_ref), (q_hbm, q_ref), (c_hbm, c_ref)]
        )
    ]
    for load in loads:
        load.start()

    def each_peer(start, cores=2):
        y = pair % Y
        columns = []
        for j in range(Z):
            z = lax.rem(pair // Y + far(j, Z), Z)
            columns += [2 * Y * z + 1 - core, 2 * Y * z + core][2 - cores :]

        def ring(i, _):
            place = 2 * lax.rem(y + far(i, Y), Y)
            for column in columns:
                start(column + place)
            return 0

        lax.fori_loop(0, Y - 1, ring, 0)
        for column in columns[:-1]:
            start(column + 2 * y)

    barrier = pltpu.get_barrier_semaphore()
    each_peer(lambda to: pl.semaphore_signal(barrier, inc=1, device_id=(to, ten), device_id_type=MESH))
    for k in range(1, T):
        pl.semaphore_signal(barrier, inc=1, device_id=(me, lax.rem(ten + k, T)), device_id_type=MESH)

    flip = exchange()

    loads[0].wait()
    taps = jnp.dot(f_ref[...], flip, preferred_element_type=F32)
    for r in range(half):
        fsend[r] = taps[r : r + 1]

    for load in loads[1:5]:
        load.wait()
    product = (k_ref[...].astype(F32) * v_ref[...].astype(F32)).astype(BF16)
    mirrored = jnp.dot(product, flip, preferred_element_type=F32).reshape(C, OWN, LANES)
    gmix = (q_ref[...].astype(F32) * c_ref[...].astype(F32)).reshape(C, OWN, LANES)
    msend[...] = jnp.concatenate([mirrored, gmix], axis=1).astype(BF16)

    pl.semaphore_wait(barrier, C - 1 + T - 1)

    def send(src, dst, phase, peer):
        return pltpu.make_async_remote_copy(
            src_ref=src, dst_ref=dst, send_sem=send_sem.at[phase], recv_sem=recv_sem.at[phase],
            device_id=peer, device_id_type=MESH,
        )

    each_peer(lambda to: send(msend.at[to], mrecv.at[me], 1, (to, ten)).start())
    each_peer(lambda to: send(fsend.at[to // 2], frecv.at[core, pair], 0, (to, ten)).start(), cores=1)

    frecv[core, pair] = fsend[pair]
    mrecv[me] = msend[me]
    toep[0] = jnp.zeros((LANES, LANES), BF16)
    z2[half * 16 :, :] = jnp.zeros((z2.shape[0] - half * 16, 2 * LANES), BF16)
    gcat[rows:, :] = jnp.zeros((gcat.shape[0] - rows, 2 * LANES), BF16)

    row = lax.broadcasted_iota(jnp.int32, (LANES, LANES), 0)
    col = lax.broadcasted_iota(jnp.int32, (LANES, LANES), 1)
    lower = col <= row

    send(mrecv.at[pl.ds(0, C - 1)], mrecv.at[pl.ds(0, C - 1)], 1, (me, ten)).wait_recv()
    zero = jnp.zeros((OWN, LANES), F32)
    other = me + 1 - 2 * core
    some_taps = frecv.at[core, pl.ds(0, half - 1)]
    send(some_taps, some_taps, 0, (me, ten)).wait_recv()
    tap_swap = send(frecv.at[core], frecv.at[core], 6, (other, ten))
    tap_swap.start()

    whole = mrecv[...].astype(F32)
    xt = whole[:, :OWN].reshape(rows, LANES).T.astype(BF16)
    gpart = whole[:, OWN:]
    after = jnp.concatenate([gpart[1:], zero[None]], axis=0)
    gcat[0:rows, :] = jnp.concatenate([gpart, after], axis=2).reshape(rows, 2 * LANES).astype(BF16)

    def lags(e, depth):
        first = pl.multiple_of(16 * e, 16)
        return jnp.dot(xt[:, :depth], gcat[pl.ds(first, depth), :], preferred_element_type=F32)

    def skew(block):
        return pltpu.roll(block, 1, 1, stride=1, stride_axis=0)

    def gather(depth, group):
        def body(n, last):
            parts = [lags(group * n + u, depth) for u in range(group)]
            for u in reversed(range(group)):
                for side in (1, 0):
                    turned = skew(parts[u][:, side * LANES : (side + 1) * LANES])
                    place = 2 * (group * n + u) + side
                    raw[place] = jnp.sum(jnp.where(lower, turned, last), axis=0, keepdims=True)
                    last = turned
            return last

        return body

    group = min(4, half // 2)
    quarter = half // 2 // group
    last = jnp.zeros((LANES, LANES), F32)
    late = gather(rows // 2, group)
    early = gather(rows, group)
    last = lax.fori_loop(0, quarter, lambda n, s: late(2 * quarter - 1 - n, s), last)
    last = lax.fori_loop(0, quarter, lambda n, s: early(quarter - 1 - n, s), last)

    swap = send(raw, raw_other, 3, (other, ten))
    swap.start()

    tap_swap.wait_recv()
    def build(n, last):
        for u in range(UNROLL):
            d = UNROLL * n + u
            turned = skew(jnp.broadcast_to(frecv[u % 2, d // 2], (LANES, LANES)))
            toep[d + 1] = jnp.where(lower, turned, last).astype(BF16)
            last = turned
        return last

    lax.fori_loop(0, C // UNROLL, build, jnp.zeros((LANES, LANES), F32))

    for j in range(half):
        two = []
        for i in (2 * j, 2 * j + 1):
            two.append(jnp.concatenate([mrecv[C - 1 - i].astype(F32)[:OWN], mrecv[i].astype(F32)[OWN:]], axis=0))
        z2[16 * j : 16 * j + 16, :] = jnp.concatenate(two, axis=1).astype(BF16)

    swap.wait_recv()
    total = raw[...] + raw_other[...]
    size2 = jnp.sum(jnp.sum(total * total, axis=0), axis=1, keepdims=True)
    size_row = jnp.broadcast_to(size2, (1, LANES))
    for i in range(C):
        gsend[i] = jnp.concatenate([total[i], size_row], axis=0)

    base = half * core
    offset = lax.rem(me, half)
    mine = core == me // half

    def send_grad(k, _):
        to = base + lax.rem(offset + k, half)
        send(gsend.at[to], grecv.at[pair], 4, (to, ten)).start()
        return 0

    lax.fori_loop(1, half, send_grad, 0)
    straight = base + offset

    @pl.when(mine)
    def _():
        grecv[pair] = gsend[me]

    @pl.when(jnp.logical_not(mine))
    def _():
        send(gsend.at[straight], grecv.at[pair], 4, (straight, ten)).start()

    def weight(d):
        top = jnp.concatenate([toep[2 * d + 1], toep[2 * d]], axis=1)
        low = jnp.concatenate([toep[2 * d + 2], toep[2 * d + 1]], axis=1)
        return jnp.concatenate([top, low], axis=0)

    step = min(4, half)
    for d0 in range(0, half, step):
        size = 16 * (half - d0)
        left = jnp.concatenate([z2[16 * (d0 + u) : 16 * (d0 + u) + size, :] for u in range(step)], axis=1)
        right = jnp.concatenate([weight(d0 + u) for u in range(step)], axis=0)
        part = jnp.dot(left, right, preferred_element_type=F32)
        if d0 == 0:
            acc[...] = part
        else:
            acc[0:size, :] += part

    for i in range(C):
        m = C - 1 - i
        conv = acc[16 * (m // 2) : 16 * (m // 2) + OWN, (m % 2) * LANES : (m % 2 + 1) * LANES]
        corr = acc[16 * (i // 2) + OWN : 16 * (i // 2) + 16, (i % 2) * LANES : (i % 2 + 1) * LANES]
        bsend[i] = jnp.concatenate([conv, corr], axis=0).astype(BF16)

    each_peer(lambda to: send(bsend.at[to], brecv.at[me], 2, (to, ten)).start())
    own_back = pltpu.make_async_copy(bsend.at[me], brecv.at[me], load_sem.at[0])
    own_back.start()

    def grads(count):
        part = pl.ds(0, count)
        return send(gsend.at[part], grecv.at[part], 4, (me, ten))

    @pl.when(mine)
    def _():
        grads(half - 1).wait_recv()

    @pl.when(jnp.logical_not(mine))
    def _():
        grads(half).wait_recv()

    square = jnp.sum(grecv[:, 1:2, :], axis=0)
    tsend[...] = square
    own_size = pltpu.make_async_copy(tsend, trecv.at[ten], load_sem.at[1])
    own_size.start()
    own_grads = pltpu.make_async_copy(grecv, grads_out, load_sem.at[2])
    own_grads.start()
    for k in range(1, T):
        send(tsend, trecv.at[ten], 5, (me, lax.rem(ten + k, T))).start()

    send(brecv.at[pl.ds(0, C - 1)], brecv.at[pl.ds(0, C - 1)], 2, (me, ten)).wait_recv()
    if T > 1:
        part = pl.ds(0, T - 1)
        send(trecv.at[part], trecv.at[part], 5, (me, ten)).wait_recv()
    own_back.wait()
    own_grads.wait()
    own_size.wait()

    send(some_taps, some_taps, 0, (me, ten)).wait_send()
    tap_swap.wait_send()
    send(msend.at[pl.ds(0, C - 1)], msend.at[pl.ds(0, C - 1)], 1, (me, ten)).wait_send()
    send(bsend.at[pl.ds(0, C - 1)], bsend.at[pl.ds(0, C - 1)], 2, (me, ten)).wait_send()
    swap.wait_send()

    @pl.when(mine)
    def _():
        grads(half - 1).wait_send()

    @pl.when(jnp.logical_not(mine))
    def _():
        grads(half).wait_send()

    if T > 1:
        part = pl.ds(0, T - 1)
        send(trecv.at[part], trecv.at[part], 5, (me, ten)).wait_send()


def gates(
    C, T, entries,
    q_hbm, k_hbm, v_hbm, c_hbm, gain_hbm, back_hbm, grads_hbm, sizes_hbm,
    mixed_hbm, gq_hbm, gk_hbm, gv_hbm, fg_hbm,
    q_ref, k_ref, v_ref, c_ref, gain_ref, back, grads, sizes,
    mixed, gq, gk, gv, fg, gain_col, load_sem, store_sem,
):
    half = C // 2
    rows = C * OWN
    pairs = [
        (q_hbm, q_ref), (k_hbm, k_ref), (v_hbm, v_ref), (c_hbm, c_ref), (back_hbm, back),
        (gain_hbm, gain_ref), (grads_hbm, grads), (sizes_hbm, sizes),
    ]
    loads = [pltpu.make_async_copy(src, dst, load_sem.at[n]) for n, (src, dst) in enumerate(pairs)]
    for load in loads:
        load.start()
    outs = [(mixed, mixed_hbm), (gq, gq_hbm), (gk, gk_hbm), (gv, gv_hbm), (fg, fg_hbm)]
    stores = [pltpu.make_async_copy(src, dst, store_sem.at[n]) for n, (src, dst) in enumerate(outs)]
    flip = exchange()
    for load in loads:
        load.wait()

    for n in range(rows // LANES):
        wide = jnp.broadcast_to(gain_ref[n : n + 1, :], (LANES, LANES))
        gain_col[n * LANES : (n + 1) * LANES, :] = wide.T
    gain = gain_col[...]
    both = back[...].astype(F32)
    conv = jnp.dot(both[:, :OWN].reshape(rows, LANES).astype(BF16), flip, preferred_element_type=F32)
    corr = both[:, OWN:].reshape(rows, LANES)
    kf = k_ref[...].astype(F32)
    vf = v_ref[...].astype(F32)
    qf = q_ref[...].astype(F32)
    cf = c_ref[...].astype(F32)
    backward = corr + gain * (qf * cf).astype(BF16).astype(F32)
    gk[...] = (backward * vf).astype(BF16)
    stores[2].start()
    gv[...] = (backward * kf).astype(BF16)
    stores[3].start()
    forward = conv + gain * (kf * vf).astype(BF16).astype(F32)
    mixed[...] = (qf * forward).astype(BF16)
    stores[0].start()
    gq[...] = (cf * forward).astype(BF16)
    stores[1].start()

    squared = jnp.sum(sizes[...], axis=0)
    factor = jnp.minimum(1.0, math.sqrt(entries) / jnp.sqrt(squared + 1e-6))
    for r in range(half):
        fg[r : r + 1, :] = grads[r, 0:1, :] * factor
    stores[4].start()
    for store in stores:
        store.wait()


def per_device(C, T, query_slab, key_slab, value_slab, cotangent, filters, skip_gain):
    channels, tokens = query_slab.shape
    half = C // 2
    rows = C * OWN
    entries = half * T * tokens * C
    gains = skip_gain.reshape(channels // LANES, LANES)
    hbm_spec = pl.BlockSpec(memory_space=pltpu.HBM)
    back = jax.ShapeDtypeStruct((C, 16, LANES), BF16)
    grads = jax.ShapeDtypeStruct((half, 2, LANES), F32)
    sizes = jax.ShapeDtypeStruct((T, 1, LANES), F32)
    came = pl.pallas_call(
        functools.partial(kernel, C, T),
        out_shape=(back, grads, sizes),
        in_specs=[hbm_spec] * 5,
        out_specs=(hbm_spec,) * 3,
        scratch_shapes=[
            pltpu.VMEM((channels, tokens), BF16),
            pltpu.VMEM((channels, tokens), BF16),
            pltpu.VMEM((channels, tokens), BF16),
            pltpu.VMEM((channels, tokens), BF16),
            pltpu.VMEM((half, tokens), BF16),
            pltpu.VMEM((half, 1, LANES), F32),
            pltpu.VMEM((2, half, 1, LANES), F32),
            pltpu.VMEM((C, 16, LANES), BF16),
            pltpu.VMEM((C, 16, LANES), BF16),
            pltpu.VMEM((C + 1, LANES, LANES), BF16),
            pltpu.VMEM((16 * (half + 4), 2 * LANES), BF16),
            pltpu.VMEM((16 * half, 2 * LANES), F32),
            pltpu.VMEM((2 * rows, 2 * LANES), BF16),
            pltpu.VMEM((C, 16, LANES), BF16),
            pltpu.VMEM((C, 1, LANES), F32),
            pltpu.VMEM((C, 1, LANES), F32),
            pltpu.VMEM((C, 2, LANES), F32),
            pltpu.VMEM((half, 2, LANES), F32),
            pltpu.VMEM((1, LANES), F32),
            pltpu.SemaphoreType.DMA((7,)),
            pltpu.SemaphoreType.DMA((7,)),
            pltpu.SemaphoreType.DMA((7,)),
        ],
        compiler_params=pltpu.CompilerParams(
            collective_id=0, has_side_effects=True, vmem_limit_bytes=VMEM_BYTES
        ),
        name="hyena",
    )(query_slab, key_slab, value_slab, cotangent, filters)
    slab = jax.ShapeDtypeStruct((channels, tokens), BF16)
    slab_buffer = pltpu.VMEM((channels, tokens), BF16)
    return pl.pallas_call(
        functools.partial(gates, C, T, entries),
        out_shape=(slab, slab, slab, slab, jax.ShapeDtypeStruct((half, tokens), F32)),
        in_specs=[hbm_spec] * 8,
        out_specs=(hbm_spec,) * 5,
        scratch_shapes=[
            slab_buffer, slab_buffer, slab_buffer, slab_buffer,
            pltpu.VMEM(gains.shape, F32),
            pltpu.VMEM(back.shape, BF16),
            pltpu.VMEM(grads.shape, F32),
            pltpu.VMEM(sizes.shape, F32),
            slab_buffer, slab_buffer, slab_buffer, slab_buffer,
            pltpu.VMEM((half, tokens), F32),
            pltpu.VMEM((channels, LANES), F32),
            pltpu.SemaphoreType.DMA((8,)),
            pltpu.SemaphoreType.DMA((5,)),
        ],
        compiler_params=pltpu.CompilerParams(vmem_limit_bytes=VMEM_BYTES),
        name="gates",
    )(query_slab, key_slab, value_slab, cotangent, gains, *came)


def solution(mesh):
    C, T = mesh.shape["context"], mesh.shape["tensor"]
    slab = P("tensor", "context")
    return jax.shard_map(
        functools.partial(per_device, C, T),
        mesh=mesh,
        in_specs=(slab, slab, slab, slab, slab, P("tensor")),
        out_specs=(slab, slab, slab, slab, slab),
        check_vma=False,
    )
```

time: 57.9 us -> 48.6 us (0.84)
  local copies, waits for them, and re-layouts: 8.21 us -> 0 us
  Pallas kernels: 48.8 us -> 47.8 us
    unnamed x17 -> x0, local copies, waits for them, and re-layouts: 8.21 us -> none
    pallas_call x1 -> x2, Pallas kernels: 48.8 us -> 47.8 us  [the longest x1 45.4 us: per_device(): pl.pallas_call(functools.partial(kernel, C, T), out_shape=(back, grads, s...]
where the time goes in v2:
time: 48.6 us; the launch traced here: 48.4 us
  Pallas kernels  47.8 us (98%)
  between operations  0.64 us (1%)
    pallas_call x1, Pallas kernels, per_device(): pl.pallas_call(functools.partial(kernel, C, T), out_shape=(back, grads, s...  45.4 us
    pallas_call x1, Pallas kernels, per_device(): pl.pallas_call(functools.partial(gates, C, T, entries), out_shape=(slab,...  2.35 us

profile of v2, /device:TPU:1, one launch (start us, length us, event | category | flops | bytes accessed | tf_op | source)
XLA Modules:
  0.0 48.4 jit_solution(6220613433390204670)
XLA Ops:
  0.6 45.4 %hyena.1 = (bf16[64,16,128]{2,1,0:T(8,128)(2,1)}, f32[32,2,128]{2,1,0:T(2,128)}, f32[8,1,128]{2,1,0:T(1,128)}) custom-call(bf16[512,128]{1,0:T(8,128)(2,1)} %q_hbm.3, bf16[512,128]{1,0:T(8,128)(2,1)} %k_hbm.3, bf16[512,128]{1,0:T(8,128)(2,1)} %v_hbm.3, bf16[512,128]{1,0:T(8,128)(2,1)} %c_hbm.3, bf16[32,128]{1,0:T(8,128)(2,1)} %f_hbm.1), custom_call_target="tpu_custom_call" | custom-call | tf_op jit(solution)/shard_map/hyena/pallas_call | solution.py:340
  46.1 2.3 %gates.1 = (bf16[512,128]{1,0:T(8,128)(2,1)}, bf16[512,128]{1,0:T(8,128)(2,1)}, bf16[512,128]{1,0:T(8,128)(2,1)}, bf16[512,128]{1,0:T(8,128)(2,1)}, f32[32,128]{1,0:T(8,128)}) custom-call(bf16[512,128]{1,0:T(8,128)(2,1)} %q_hbm.3, bf16[512,128]{1,0:T(8,128)(2,1)} %k_hbm.3, bf16[512,128]{1,0:T(8,128)(2,1)} %v_hbm.3, bf16[512,128]{1,0:T(8,128)(2,1)} %c_hbm.3, ...), custom_call_target="tpu_custom_call" | custom-call | tf_op jit(solution)/shard_map/gates/pallas_call | solution.py:376

commit v3 on v2

--- a/solution.py
+++ b/solution.py
@@ -30,18 +30,19 @@
 def kernel(
     C, T,
     q_hbm, k_hbm, v_hbm, c_hbm, f_hbm,
-    brecv, grads_out, trecv,
+    back_hbm, grads_hbm,
     q_ref, k_ref, v_ref, c_ref, f_ref,
     fsend, frecv, msend, mrecv, toep, z2, acc, gcat, bsend,
-    raw, raw_other, gsend, grecv, tsend,
+    raw, raw_other, gsend, tsend, trecv,
     load_sem, send_sem, recv_sem,
 ):
     me = lax.axis_index("context")
     ten = lax.axis_index("tensor")
     half = C // 2
-    Z = max(1, C // 16)
-    Y = half // Z
+    Z, Y = 4, C // 8
     pair = me // 2
+    z = pair // Y
+    y = pair % Y
     core = me % 2
     rows = C * OWN
 
@@ -55,21 +56,31 @@
         load.start()
 
     def each_peer(start, cores=2):
-        y = pair % Y
         columns = []
         for j in range(Z):
-            z = lax.rem(pair // Y + far(j, Z), Z)
-            columns += [2 * Y * z + 1 - core, 2 * Y * z + core][2 - cores :]
-
-        def ring(i, _):
+            plane = lax.rem(z + far(j, Z), Z)
+            columns += [2 * Y * plane + 1 - core, 2 * Y * plane + core][2 - cores :]
+        ring(start, columns, False)
+
+    def ring(start, columns, last):
+        def at(i, _):
             place = 2 * lax.rem(y + far(i, Y), Y)
             for column in columns:
                 start(column + place)
             return 0
 
-        lax.fori_loop(0, Y - 1, ring, 0)
+        lax.fori_loop(0, Y - 1, at, 0)
         for column in columns[:-1]:
             start(column + 2 * y)
+        if last is not False:
+            pl.when(last)(lambda: start(columns[-1] + 2 * y))
+
+    def half_peers(start, late, cores=2):
+        one = lax.rem((z + 1) // 2 + 1 - late, 2)
+        columns = []
+        for plane in (2 * late + one, 2 * late + 1 - one):
+            columns += [2 * Y * plane + 1 - core, 2 * Y * plane + core][2 - cores :]
+        ring(start, columns, z // 2 != late)
 
     barrier = pltpu.get_barrier_semaphore()
     each_peer(lambda to: pl.semaphore_signal(barrier, inc=1, device_id=(to, ten), device_id_type=MESH))
@@ -98,8 +109,12 @@
             device_id=peer, device_id_type=MESH,
         )
 
-    each_peer(lambda to: send(msend.at[to], mrecv.at[me], 1, (to, ten)).start())
     each_peer(lambda to: send(fsend.at[to // 2], frecv.at[core, pair], 0, (to, ten)).start(), cores=1)
+
+    def send_main(to):
+        send(msend.at[to], mrecv.at[me], 1, (to, ten)).start()
+
+    each_peer(send_main)
 
     frecv[core, pair] = fsend[pair]
     mrecv[me] = msend[me]
@@ -111,14 +126,28 @@
     col = lax.broadcasted_iota(jnp.int32, (LANES, LANES), 1)
     lower = col <= row
 
-    send(mrecv.at[pl.ds(0, C - 1)], mrecv.at[pl.ds(0, C - 1)], 1, (me, ten)).wait_recv()
-    zero = jnp.zeros((OWN, LANES), F32)
+    def skew(block):
+        return pltpu.roll(block, 1, 1, stride=1, stride_axis=0)
+
     other = me + 1 - 2 * core
     some_taps = frecv.at[core, pl.ds(0, half - 1)]
     send(some_taps, some_taps, 0, (me, ten)).wait_recv()
     tap_swap = send(frecv.at[core], frecv.at[core], 6, (other, ten))
     tap_swap.start()
 
+    tap_swap.wait_recv()
+    def build(n, last):
+        for u in range(UNROLL):
+            d = UNROLL * n + u
+            turned = skew(jnp.broadcast_to(frecv[u % 2, d // 2], (LANES, LANES)))
+            toep[d + 1] = jnp.where(lower, turned, last).astype(BF16)
+            last = turned
+        return last
+
+    lax.fori_loop(0, C // UNROLL, build, jnp.zeros((LANES, LANES), F32))
+
+    send(mrecv.at[pl.ds(0, C - 1)], mrecv.at[pl.ds(0, C - 1)], 1, (me, ten)).wait_recv()
+    zero = jnp.zeros((OWN, LANES), F32)
     whole = mrecv[...].astype(F32)
     xt = whole[:, :OWN].reshape(rows, LANES).T.astype(BF16)
     gpart = whole[:, OWN:]
@@ -128,9 +157,6 @@
     def lags(e, depth):
         first = pl.multiple_of(16 * e, 16)
         return jnp.dot(xt[:, :depth], gcat[pl.ds(first, depth), :], preferred_element_type=F32)
-
-    def skew(block):
-        return pltpu.roll(block, 1, 1, stride=1, stride_axis=0)
 
     def gather(depth, group):
         def body(n, last):
@@ -145,27 +171,14 @@
 
         return body
 
-    group = min(4, half // 2)
-    quarter = half // 2 // group
+    group = min(8, half // 2)
     last = jnp.zeros((LANES, LANES), F32)
-    late = gather(rows // 2, group)
-    early = gather(rows, group)
-    last = lax.fori_loop(0, quarter, lambda n, s: late(2 * quarter - 1 - n, s), last)
-    last = lax.fori_loop(0, quarter, lambda n, s: early(quarter - 1 - n, s), last)
+    for n in reversed(range(half // group)):
+        depth = rows if 2 * group * n < half else rows // 2
+        last = gather(depth, group)(n, last)
 
     swap = send(raw, raw_other, 3, (other, ten))
     swap.start()
-
-    tap_swap.wait_recv()
-    def build(n, last):
-        for u in range(UNROLL):
-            d = UNROLL * n + u
-            turned = skew(jnp.broadcast_to(frecv[u % 2, d // 2], (LANES, LANES)))
-            toep[d + 1] = jnp.where(lower, turned, last).astype(BF16)
-            last = turned
-        return last
-
-    lax.fori_loop(0, C // UNROLL, build, jnp.zeros((LANES, LANES), F32))
 
     for j in range(half):
         two = []
@@ -175,30 +188,11 @@
 
     swap.wait_recv()
     total = raw[...] + raw_other[...]
-    size2 = jnp.sum(jnp.sum(total * total, axis=0), axis=1, keepdims=True)
-    size_row = jnp.broadcast_to(size2, (1, LANES))
-    for i in range(C):
-        gsend[i] = jnp.concatenate([total[i], size_row], axis=0)
-
-    base = half * core
-    offset = lax.rem(me, half)
-    mine = core == me // half
-
-    def send_grad(k, _):
-        to = base + lax.rem(offset + k, half)
-        send(gsend.at[to], grecv.at[pair], 4, (to, ten)).start()
-        return 0
-
-    lax.fori_loop(1, half, send_grad, 0)
-    straight = base + offset
-
-    @pl.when(mine)
-    def _():
-        grecv[pair] = gsend[me]
-
-    @pl.when(jnp.logical_not(mine))
-    def _():
-        send(gsend.at[straight], grecv.at[pair], 4, (straight, ten)).start()
+    size = jnp.broadcast_to(jnp.sum(jnp.sum(total * total, axis=0), axis=1, keepdims=True), (1, LANES))
+    tsend[...] = size
+    trecv[ten] = size
+    for k in range(1, T):
+        send(tsend, trecv.at[ten], 5, (me, lax.rem(ten + k, T))).start()
 
     def weight(d):
         top = jnp.concatenate([toep[2 * d + 1], toep[2 * d]], axis=1)
@@ -222,38 +216,34 @@
         corr = acc[16 * (i // 2) + OWN : 16 * (i // 2) + 16, (i % 2) * LANES : (i % 2 + 1) * LANES]
         bsend[i] = jnp.concatenate([conv, corr], axis=0).astype(BF16)
 
-    each_peer(lambda to: send(bsend.at[to], brecv.at[me], 2, (to, ten)).start())
-    own_back = pltpu.make_async_copy(bsend.at[me], brecv.at[me], load_sem.at[0])
-    own_back.start()
-
-    def grads(count):
-        part = pl.ds(0, count)
-        return send(gsend.at[part], grecv.at[part], 4, (me, ten))
-
-    @pl.when(mine)
-    def _():
-        grads(half - 1).wait_recv()
-
-    @pl.when(jnp.logical_not(mine))
-    def _():
-        grads(half).wait_recv()
-
-    square = jnp.sum(grecv[:, 1:2, :], axis=0)
-    tsend[...] = square
-    own_size = pltpu.make_async_copy(tsend, trecv.at[ten], load_sem.at[1])
-    own_size.start()
-    own_grads = pltpu.make_async_copy(grecv, grads_out, load_sem.at[2])
-    own_grads.start()
-    for k in range(1, T):
-        send(tsend, trecv.at[ten], 5, (me, lax.rem(ten + k, T))).start()
-
-    send(brecv.at[pl.ds(0, C - 1)], brecv.at[pl.ds(0, C - 1)], 2, (me, ten)).wait_recv()
+    def send_back(to):
+        send(bsend.at[to], back_hbm.at[me], 2, (to, ten)).start()
+
+    def send_grad(to):
+        send(gsend.at[to], grads_hbm.at[pair], 4, (to, ten)).start()
+
+    half_peers(send_back, 0)
+
     if T > 1:
         part = pl.ds(0, T - 1)
         send(trecv.at[part], trecv.at[part], 5, (me, ten)).wait_recv()
+    square = jnp.sum(trecv[...], axis=0)
+    for i in range(C):
+        gsend[i] = jnp.concatenate([raw[i] + raw_other[i], square], axis=0)
+    half_peers(send_grad, 0, cores=1)
+    half_peers(send_back, 1)
+    half_peers(send_grad, 1, cores=1)
+    own_back = pltpu.make_async_copy(bsend.at[me], back_hbm.at[me], load_sem.at[0])
+    own_grad = pltpu.make_async_copy(gsend.at[me], grads_hbm.at[pair], load_sem.at[1])
+    own_back.start()
+    own_grad.start()
+
+    some_back = back_hbm.at[pl.ds(0, C - 1)]
+    send(some_back, some_back, 2, (me, ten)).wait_recv()
+    some_grads = grads_hbm.at[pl.ds(0, half - 1)]
+    send(some_grads, some_grads, 4, (me, ten)).wait_recv()
     own_back.wait()
-    own_grads.wait()
-    own_size.wait()
+    own_grad.wait()
 
     send(some_taps, some_taps, 0, (me, ten)).wait_send()
     tap_swap.wait_send()
@@ -261,31 +251,24 @@
     send(bsend.at[pl.ds(0, C - 1)], bsend.at[pl.ds(0, C - 1)], 2, (me, ten)).wait_send()
     swap.wait_send()
 
-    @pl.when(mine)
-    def _():
-        grads(half - 1).wait_send()
-
-    @pl.when(jnp.logical_not(mine))
-    def _():
-        grads(half).wait_send()
-
+    send(some_grads, some_grads, 4, (me, ten)).wait_send()
     if T > 1:
         part = pl.ds(0, T - 1)
         send(trecv.at[part], trecv.at[part], 5, (me, ten)).wait_send()
 
 
 def gates(
-    C, T, entries,
-    q_hbm, k_hbm, v_hbm, c_hbm, gain_hbm, back_hbm, grads_hbm, sizes_hbm,
+    C, entries,
+    q_hbm, k_hbm, v_hbm, c_hbm, gain_hbm, back_hbm, grads_hbm,
     mixed_hbm, gq_hbm, gk_hbm, gv_hbm, fg_hbm,
-    q_ref, k_ref, v_ref, c_ref, gain_ref, back, grads, sizes,
+    q_ref, k_ref, v_ref, c_ref, gain_ref, back, grads,
     mixed, gq, gk, gv, fg, gain_col, load_sem, store_sem,
 ):
     half = C // 2
     rows = C * OWN
     pairs = [
         (q_hbm, q_ref), (k_hbm, k_ref), (v_hbm, v_ref), (c_hbm, c_ref), (back_hbm, back),
-        (gain_hbm, gain_ref), (grads_hbm, grads), (sizes_hbm, sizes),
+        (gain_hbm, gain_ref), (grads_hbm, grads),
     ]
     loads = [pltpu.make_async_copy(src, dst, load_sem.at[n]) for n, (src, dst) in enumerate(pairs)]
     for load in loads:
@@ -318,7 +301,7 @@
     gq[...] = (cf * forward).astype(BF16)
     stores[1].start()
 
-    squared = jnp.sum(sizes[...], axis=0)
+    squared = jnp.sum(grads[:, 1:2, :], axis=0)
     factor = jnp.minimum(1.0, math.sqrt(entries) / jnp.sqrt(squared + 1e-6))
     for r in range(half):
         fg[r : r + 1, :] = grads[r, 0:1, :] * factor
@@ -336,12 +319,11 @@
     hbm_spec = pl.BlockSpec(memory_space=pltpu.HBM)
     back = jax.ShapeDtypeStruct((C, 16, LANES), BF16)
     grads = jax.ShapeDtypeStruct((half, 2, LANES), F32)
-    sizes = jax.ShapeDtypeStruct((T, 1, LANES), F32)
     came = pl.pallas_call(
         functools.partial(kernel, C, T),
-        out_shape=(back, grads, sizes),
+        out_shape=(back, grads),
         in_specs=[hbm_spec] * 5,
-        out_specs=(hbm_spec,) * 3,
+        out_specs=(hbm_spec,) * 2,
         scratch_shapes=[
             pltpu.VMEM((channels, tokens), BF16),
             pltpu.VMEM((channels, tokens), BF16),
@@ -360,8 +342,8 @@
             pltpu.VMEM((C, 1, LANES), F32),
             pltpu.VMEM((C, 1, LANES), F32),
             pltpu.VMEM((C, 2, LANES), F32),
-            pltpu.VMEM((half, 2, LANES), F32),
             pltpu.VMEM((1, LANES), F32),
+            pltpu.VMEM((T, 1, LANES), F32),
             pltpu.SemaphoreType.DMA((7,)),
             pltpu.SemaphoreType.DMA((7,)),
             pltpu.SemaphoreType.DMA((7,)),
@@ -374,20 +356,19 @@
     slab = jax.ShapeDtypeStruct((channels, tokens), BF16)
     slab_buffer = pltpu.VMEM((channels, tokens), BF16)
     return pl.pallas_call(
-        functools.partial(gates, C, T, entries),
+        functools.partial(gates, C, entries),
         out_shape=(slab, slab, slab, slab, jax.ShapeDtypeStruct((half, tokens), F32)),
-        in_specs=[hbm_spec] * 8,
+        in_specs=[hbm_spec] * 7,
         out_specs=(hbm_spec,) * 5,
         scratch_shapes=[
             slab_buffer, slab_buffer, slab_buffer, slab_buffer,
             pltpu.VMEM(gains.shape, F32),
             pltpu.VMEM(back.shape, BF16),
             pltpu.VMEM(grads.shape, F32),
-            pltpu.VMEM(sizes.shape, F32),
             slab_buffer, slab_buffer, slab_buffer, slab_buffer,
             pltpu.VMEM((half, tokens), F32),
             pltpu.VMEM((channels, LANES), F32),
-            pltpu.SemaphoreType.DMA((8,)),
+            pltpu.SemaphoreType.DMA((7,)),
             pltpu.SemaphoreType.DMA((5,)),
         ],
         compiler_params=pltpu.CompilerParams(vmem_limit_bytes=VMEM_BYTES),

time: 48.6 us -> 44.4 us (0.914)
  Pallas kernels: 47.8 us -> 43.6 us
    pallas_call x2, Pallas kernels: 47.8 us -> 43.6 us  [the longest x1 41.3 us: per_device(): pl.pallas_call(functools.partial(kernel, C, T), out_shape=(back, grads),...]
where the time goes in v3:
time: 44.4 us; the launch traced here: 44.3 us
  Pallas kernels  43.6 us (98%)
  between operations  0.64 us (1%)
    pallas_call x1, Pallas kernels, per_device(): pl.pallas_call(functools.partial(kernel, C, T), out_shape=(back, grads),...  41.3 us
    pallas_call x1, Pallas kernels, per_device(): pl.pallas_call(functools.partial(gates, C, entries), out_shape=(slab, sla...  2.34 us

profile of v3, /device:TPU:1, one launch (start us, length us, event | category | flops | bytes accessed | tf_op | source)
XLA Modules:
  0.0 44.3 jit_solution(12916047275255741680)
XLA Ops:
  0.6 41.3 %hyena.1 = (bf16[64,16,128]{2,1,0:T(8,128)(2,1)}, f32[32,2,128]{2,1,0:T(2,128)}) custom-call(bf16[512,128]{1,0:T(8,128)(2,1)} %q_hbm.3, bf16[512,128]{1,0:T(8,128)(2,1)} %k_hbm.3, bf16[512,128]{1,0:T(8,128)(2,1)} %v_hbm.3, bf16[512,128]{1,0:T(8,128)(2,1)} %c_hbm.3, bf16[32,128]{1,0:T(8,128)(2,1)} %f_hbm.1), custom_call_target="tpu_custom_call" | custom-call | tf_op jit(solution)/shard_map/hyena/pallas_call | solution.py:322
  41.9 2.3 %gates.1 = (bf16[512,128]{1,0:T(8,128)(2,1)}, bf16[512,128]{1,0:T(8,128)(2,1)}, bf16[512,128]{1,0:T(8,128)(2,1)}, bf16[512,128]{1,0:T(8,128)(2,1)}, f32[32,128]{1,0:T(8,128)}) custom-call(bf16[512,128]{1,0:T(8,128)(2,1)} %q_hbm.3, bf16[512,128]{1,0:T(8,128)(2,1)} %k_hbm.3, bf16[512,128]{1,0:T(8,128)(2,1)} %v_hbm.3, bf16[512,128]{1,0:T(8,128)(2,1)} %c_hbm.3, ...), custom_call_target="tpu_custom_call" | custom-call | tf_op jit(solution)/shard_map/gates/pallas_call | solution.py:358

commit v4 on v3

--- a/solution.py
+++ b/solution.py
@@ -12,7 +12,7 @@
 F32 = jnp.float32
 BF16 = jnp.bfloat16
 LANES = 128
-VMEM_BYTES = 62 * 1024 * 1024
+VMEM_BYTES = 32 * 1024 * 1024
 UNROLL = 8
 OWN = 8
 
@@ -29,11 +29,11 @@
 
 def kernel(
     C, T,
-    q_hbm, k_hbm, v_hbm, c_hbm, f_hbm,
-    back_hbm, grads_hbm,
-    q_ref, k_ref, v_ref, c_ref, f_ref,
+    q_hbm, k_hbm, v_hbm, c_hbm, f_hbm, gain_hbm,
+    back, grads, sizes, q_ref, k_ref, v_ref, c_ref, scaled_product, scaled_gmix,
+    f_ref, gain_ref,
     fsend, frecv, msend, mrecv, toep, z2, acc, gcat, bsend,
-    raw, raw_other, gsend, tsend, trecv,
+    raw, raw_other, gsend, tsend,
     load_sem, send_sem, recv_sem,
 ):
     me = lax.axis_index("context")
@@ -46,15 +46,6 @@
     core = me % 2
     rows = C * OWN
 
-    loads = [
-        pltpu.make_async_copy(src, dst, load_sem.at[n])
-        for n, (src, dst) in enumerate(
-            [(f_hbm, f_ref), (k_hbm, k_ref), (v_hbm, v_ref), (q_hbm, q_ref), (c_hbm, c_ref)]
-        )
-    ]
-    for load in loads:
-        load.start()
-
     def each_peer(start, cores=2):
         columns = []
         for j in range(Z):
@@ -87,6 +78,15 @@
     for k in range(1, T):
         pl.semaphore_signal(barrier, inc=1, device_id=(me, lax.rem(ten + k, T)), device_id_type=MESH)
 
+    loads = [
+        pltpu.make_async_copy(src, dst, load_sem.at[n])
+        for n, (src, dst) in enumerate(
+            [(f_hbm, f_ref), (k_hbm, k_ref), (v_hbm, v_ref), (q_hbm, q_ref), (c_hbm, c_ref), (gain_hbm, gain_ref)]
+        )
+    ]
+    for load in loads:
+        load.start()
+
     flip = exchange()
 
     loads[0].wait()
@@ -109,15 +109,25 @@
             device_id=peer, device_id_type=MESH,
         )
 
-    each_peer(lambda to: send(fsend.at[to // 2], frecv.at[core, pair], 0, (to, ten)).start(), cores=1)
-
     def send_main(to):
         send(msend.at[to], mrecv.at[me], 1, (to, ten)).start()
 
+    def send_taps(to):
+        send(fsend.at[to // 2], frecv.at[core, pair], 0, (to, ten)).start()
+
+    each_peer(send_taps, cores=1)
     each_peer(send_main)
 
     frecv[core, pair] = fsend[pair]
     mrecv[me] = msend[me]
+    loads[5].wait()
+    for n in range(rows // LANES):
+        lines = slice(n * LANES, (n + 1) * LANES)
+        gain = jnp.broadcast_to(gain_ref[n : n + 1, :], (LANES, LANES)).T
+        part = (k_ref[lines].astype(F32) * v_ref[lines].astype(F32)).astype(BF16)
+        scaled_product[lines] = gain * part.astype(F32)
+        part = (q_ref[lines].astype(F32) * c_ref[lines].astype(F32)).astype(BF16)
+        scaled_gmix[lines] = gain * part.astype(F32)
     toep[0] = jnp.zeros((LANES, LANES), BF16)
     z2[half * 16 :, :] = jnp.zeros((z2.shape[0] - half * 16, 2 * LANES), BF16)
     gcat[rows:, :] = jnp.zeros((gcat.shape[0] - rows, 2 * LANES), BF16)
@@ -189,10 +199,14 @@
     swap.wait_recv()
     total = raw[...] + raw_other[...]
     size = jnp.broadcast_to(jnp.sum(jnp.sum(total * total, axis=0), axis=1, keepdims=True), (1, LANES))
-    tsend[...] = size
-    trecv[ten] = size
-    for k in range(1, T):
-        send(tsend, trecv.at[ten], 5, (me, lax.rem(ten + k, T))).start()
+    gsend[:, 0:1, :] = total
+    gsend[:, 1:2, :] = jnp.broadcast_to(size[None], (C, 1, LANES))
+
+    def send_grad(to):
+        send(gsend.at[to], grads.at[pair], 4, (to, ten)).start()
+
+    half_peers(send_grad, 0, cores=1)
+    grads[pair] = gsend[me]
 
     def weight(d):
         top = jnp.concatenate([toep[2 * d + 1], toep[2 * d]], axis=1)
@@ -217,33 +231,26 @@
         bsend[i] = jnp.concatenate([conv, corr], axis=0).astype(BF16)
 
     def send_back(to):
-        send(bsend.at[to], back_hbm.at[me], 2, (to, ten)).start()
-
-    def send_grad(to):
-        send(gsend.at[to], grads_hbm.at[pair], 4, (to, ten)).start()
+        send(bsend.at[to], back.at[me], 2, (to, ten)).start()
 
     half_peers(send_back, 0)
-
+    half_peers(send_grad, 1, cores=1)
+    half_peers(send_back, 1)
+    back[me] = bsend[me]
+
+    some_grads = grads.at[pl.ds(0, half - 1)]
+    send(some_grads, some_grads, 4, (me, ten)).wait_recv()
+    square = jnp.sum(grads[:, 1:2, :], axis=0)
+    tsend[...] = square
+    for k in range(1, T):
+        send(tsend, sizes.at[ten], 5, (me, lax.rem(ten + k, T))).start()
+    sizes[ten] = square
+
+    some_back = back.at[pl.ds(0, C - 1)]
+    send(some_back, some_back, 2, (me, ten)).wait_recv()
     if T > 1:
         part = pl.ds(0, T - 1)
-        send(trecv.at[part], trecv.at[part], 5, (me, ten)).wait_recv()
-    square = jnp.sum(trecv[...], axis=0)
-    for i in range(C):
-        gsend[i] = jnp.concatenate([raw[i] + raw_other[i], square], axis=0)
-    half_peers(send_grad, 0, cores=1)
-    half_peers(send_back, 1)
-    half_peers(send_grad, 1, cores=1)
-    own_back = pltpu.make_async_copy(bsend.at[me], back_hbm.at[me], load_sem.at[0])
-    own_grad = pltpu.make_async_copy(gsend.at[me], grads_hbm.at[pair], load_sem.at[1])
-    own_back.start()
-    own_grad.start()
-
-    some_back = back_hbm.at[pl.ds(0, C - 1)]
-    send(some_back, some_back, 2, (me, ten)).wait_recv()
-    some_grads = grads_hbm.at[pl.ds(0, half - 1)]
-    send(some_grads, some_grads, 4, (me, ten)).wait_recv()
-    own_back.wait()
-    own_grad.wait()
+        send(sizes.at[part], sizes.at[part], 5, (me, ten)).wait_recv()
 
     send(some_taps, some_taps, 0, (me, ten)).wait_send()
     tap_swap.wait_send()
@@ -254,54 +261,33 @@
     send(some_grads, some_grads, 4, (me, ten)).wait_send()
     if T > 1:
         part = pl.ds(0, T - 1)
-        send(trecv.at[part], trecv.at[part], 5, (me, ten)).wait_send()
+        send(sizes.at[part], sizes.at[part], 5, (me, ten)).wait_send()
 
 
 def gates(
     C, entries,
-    q_hbm, k_hbm, v_hbm, c_hbm, gain_hbm, back_hbm, grads_hbm,
+    back, grads, sizes, q_ref, k_ref, v_ref, c_ref, scaled_product, scaled_gmix,
     mixed_hbm, gq_hbm, gk_hbm, gv_hbm, fg_hbm,
-    q_ref, k_ref, v_ref, c_ref, gain_ref, back, grads,
-    mixed, gq, gk, gv, fg, gain_col, load_sem, store_sem,
+    mixed, gq, gk, gv, fg, store_sem,
 ):
     half = C // 2
     rows = C * OWN
-    pairs = [
-        (q_hbm, q_ref), (k_hbm, k_ref), (v_hbm, v_ref), (c_hbm, c_ref), (back_hbm, back),
-        (gain_hbm, gain_ref), (grads_hbm, grads),
-    ]
-    loads = [pltpu.make_async_copy(src, dst, load_sem.at[n]) for n, (src, dst) in enumerate(pairs)]
-    for load in loads:
-        load.start()
     outs = [(mixed, mixed_hbm), (gq, gq_hbm), (gk, gk_hbm), (gv, gv_hbm), (fg, fg_hbm)]
     stores = [pltpu.make_async_copy(src, dst, store_sem.at[n]) for n, (src, dst) in enumerate(outs)]
-    flip = exchange()
-    for load in loads:
-        load.wait()
-
-    for n in range(rows // LANES):
-        wide = jnp.broadcast_to(gain_ref[n : n + 1, :], (LANES, LANES))
-        gain_col[n * LANES : (n + 1) * LANES, :] = wide.T
-    gain = gain_col[...]
     both = back[...].astype(F32)
-    conv = jnp.dot(both[:, :OWN].reshape(rows, LANES).astype(BF16), flip, preferred_element_type=F32)
-    corr = both[:, OWN:].reshape(rows, LANES)
-    kf = k_ref[...].astype(F32)
-    vf = v_ref[...].astype(F32)
-    qf = q_ref[...].astype(F32)
-    cf = c_ref[...].astype(F32)
-    backward = corr + gain * (qf * cf).astype(BF16).astype(F32)
-    gk[...] = (backward * vf).astype(BF16)
+    backward = both[:, OWN:].reshape(rows, LANES) + scaled_gmix[...]
+    gk[...] = (backward * v_ref[...].astype(F32)).astype(BF16)
     stores[2].start()
-    gv[...] = (backward * kf).astype(BF16)
+    gv[...] = (backward * k_ref[...].astype(F32)).astype(BF16)
     stores[3].start()
-    forward = conv + gain * (kf * vf).astype(BF16).astype(F32)
-    mixed[...] = (qf * forward).astype(BF16)
+    conv = jnp.dot(both[:, :OWN].reshape(rows, LANES).astype(BF16), exchange(), preferred_element_type=F32)
+    forward = conv + scaled_product[...]
+    mixed[...] = (q_ref[...].astype(F32) * forward).astype(BF16)
     stores[0].start()
-    gq[...] = (cf * forward).astype(BF16)
+    gq[...] = (c_ref[...].astype(F32) * forward).astype(BF16)
     stores[1].start()
 
-    squared = jnp.sum(grads[:, 1:2, :], axis=0)
+    squared = jnp.sum(sizes[...], axis=0)
     factor = jnp.minimum(1.0, math.sqrt(entries) / jnp.sqrt(squared + 1e-6))
     for r in range(half):
         fg[r : r + 1, :] = grads[r, 0:1, :] * factor
@@ -317,19 +303,24 @@
     entries = half * T * tokens * C
     gains = skip_gain.reshape(channels // LANES, LANES)
     hbm_spec = pl.BlockSpec(memory_space=pltpu.HBM)
-    back = jax.ShapeDtypeStruct((C, 16, LANES), BF16)
-    grads = jax.ShapeDtypeStruct((half, 2, LANES), F32)
-    came = pl.pallas_call(
+    slab = jax.ShapeDtypeStruct((channels, tokens), BF16)
+    kept_slab = pltpu.VMEM((channels, tokens), BF16)
+    kept_scaled = pltpu.VMEM((channels, tokens), F32)
+    vmem_spec = pl.BlockSpec(memory_space=pltpu.VMEM)
+    inputs = (query_slab, key_slab, value_slab, cotangent, filters, gains)
+    kept = pl.pallas_call(
         functools.partial(kernel, C, T),
-        out_shape=(back, grads),
-        in_specs=[hbm_spec] * 5,
-        out_specs=(hbm_spec,) * 2,
+        out_shape=(
+            pltpu.VMEM((C, 16, LANES), BF16),
+            pltpu.VMEM((half, 2, LANES), F32),
+            pltpu.VMEM((T, 1, LANES), F32),
+            kept_slab, kept_slab, kept_slab, kept_slab, kept_scaled, kept_scaled,
+        ),
+        in_specs=[hbm_spec] * 6,
+        out_specs=(vmem_spec,) * 9,
         scratch_shapes=[
-            pltpu.VMEM((channels, tokens), BF16),
-            pltpu.VMEM((channels, tokens), BF16),
-            pltpu.VMEM((channels, tokens), BF16),
-            pltpu.VMEM((channels, tokens), BF16),
             pltpu.VMEM((half, tokens), BF16),
+            pltpu.VMEM(gains.shape, F32),
             pltpu.VMEM((half, 1, LANES), F32),
             pltpu.VMEM((2, half, 1, LANES), F32),
             pltpu.VMEM((C, 16, LANES), BF16),
@@ -343,7 +334,6 @@
             pltpu.VMEM((C, 1, LANES), F32),
             pltpu.VMEM((C, 2, LANES), F32),
             pltpu.VMEM((1, LANES), F32),
-            pltpu.VMEM((T, 1, LANES), F32),
             pltpu.SemaphoreType.DMA((7,)),
             pltpu.SemaphoreType.DMA((7,)),
             pltpu.SemaphoreType.DMA((7,)),
@@ -352,28 +342,21 @@
             collective_id=0, has_side_effects=True, vmem_limit_bytes=VMEM_BYTES
         ),
         name="hyena",
-    )(query_slab, key_slab, value_slab, cotangent, filters)
-    slab = jax.ShapeDtypeStruct((channels, tokens), BF16)
+    )(*(pltpu.with_memory_space_constraint(array, pltpu.HBM) for array in inputs))
     slab_buffer = pltpu.VMEM((channels, tokens), BF16)
     return pl.pallas_call(
         functools.partial(gates, C, entries),
         out_shape=(slab, slab, slab, slab, jax.ShapeDtypeStruct((half, tokens), F32)),
-        in_specs=[hbm_spec] * 7,
+        in_specs=[vmem_spec] * 9,
         out_specs=(hbm_spec,) * 5,
         scratch_shapes=[
             slab_buffer, slab_buffer, slab_buffer, slab_buffer,
-            pltpu.VMEM(gains.shape, F32),
-            pltpu.VMEM(back.shape, BF16),
-            pltpu.VMEM(grads.shape, F32),
-            slab_buffer, slab_buffer, slab_buffer, slab_buffer,
             pltpu.VMEM((half, tokens), F32),
-            pltpu.VMEM((channels, LANES), F32),
-            pltpu.SemaphoreType.DMA((7,)),
             pltpu.SemaphoreType.DMA((5,)),
         ],
         compiler_params=pltpu.CompilerParams(vmem_limit_bytes=VMEM_BYTES),
         name="gates",
-    )(query_slab, key_slab, value_slab, cotangent, gains, *came)
+    )(*(pltpu.with_memory_space_constraint(array, pltpu.VMEM) for array in kept))
 
 
 def solution(mesh):

time: 44.4 us -> 42.6 us (0.959)
  Pallas kernels: 43.6 us -> 41.9 us
    pallas_call x1, Pallas kernels: 2.34 us -> 1.04 us  [per_device(): pl.pallas_call(functools.partial(gates, C, entries), out_shape=(slab, sla...]
    pallas_call x1, Pallas kernels: 41.3 us -> 40.8 us  [per_device(): pl.pallas_call(functools.partial(kernel, C, T), out_shape=(pltpu.VMEM((C,...]
where the time goes in v4:
time: 42.6 us; the launch traced here: 42.5 us
  Pallas kernels  41.9 us (98%)
  between operations  0.64 us (2%)
    pallas_call x1, Pallas kernels, per_device(): pl.pallas_call(functools.partial(kernel, C, T), out_shape=(pltpu.VMEM((C,...  40.8 us
    pallas_call x1, Pallas kernels, per_device(): pl.pallas_call(functools.partial(gates, C, entries), out_shape=(slab, sla...  1.04 us

profile of v4, /device:TPU:1, one launch (start us, length us, event | category | flops | bytes accessed | tf_op | source)
XLA Modules:
  0.0 42.5 jit_solution(18096526433077770244)
XLA Ops:
  0.6 40.8 %hyena.1 = (bf16[64,16,128]{2,1,0:T(8,128)(2,1)S(1)}, f32[32,2,128]{2,1,0:T(2,128)S(1)}, f32[8,1,128]{2,1,0:T(1,128)S(1)}, bf16[512,128]{1,0:T(8,128)(2,1)S(1)},...) custom-call(bf16[512,128]{1,0:T(8,128)(2,1)} %q_hbm.1, ...), custom_call_target="tpu_custom_call" | custom-call | tf_op jit(solution)/shard_map/hyena/pallas_call | solution.py:311
  41.5 1.0 %gates.1 = (bf16[512,128]{1,0:T(8,128)(2,1)}, bf16[512,128]{1,0:T(8,128)(2,1)}, bf16[512,128]{1,0:T(8,128)(2,1)}, bf16[512,128]{1,0:T(8,128)(2,1)}, f32[32,128]{1,0:T(8,128)}) custom-call(bf16[64,16,128]{2,1,0:T(8,128)(2,1)S(1)} %get-tuple-element.14.back, f32[32,2,128]{2,1,0:T(2,128)S(1)} %get-tuple-element.15.grads, ...), custom_call_target="tpu_custom_call" | custom-call | tf_op jit(solution)/shard_map/gates/pallas_call | solution.py:347

commit v5 on v4

--- a/solution.py
+++ b/solution.py
@@ -13,7 +13,7 @@
 BF16 = jnp.bfloat16
 LANES = 128
 VMEM_BYTES = 32 * 1024 * 1024
-UNROLL = 8
+UNROLL = 16
 OWN = 8
 
 
@@ -198,7 +198,7 @@
 
     swap.wait_recv()
     total = raw[...] + raw_other[...]
-    size = jnp.broadcast_to(jnp.sum(jnp.sum(total * total, axis=0), axis=1, keepdims=True), (1, LANES))
+    size = jnp.sum(total * total, axis=0)
     gsend[:, 0:1, :] = total
     gsend[:, 1:2, :] = jnp.broadcast_to(size[None], (C, 1, LANES))
 
@@ -274,6 +274,8 @@
     rows = C * OWN
     outs = [(mixed, mixed_hbm), (gq, gq_hbm), (gk, gk_hbm), (gv, gv_hbm), (fg, fg_hbm)]
     stores = [pltpu.make_async_copy(src, dst, store_sem.at[n]) for n, (src, dst) in enumerate(outs)]
+    squared = jnp.sum(jnp.sum(sizes[...], axis=0), axis=1, keepdims=True)
+    factor = jnp.minimum(1.0, math.sqrt(entries) / jnp.sqrt(squared + 1e-6))
     both = back[...].astype(F32)
     backward = both[:, OWN:].reshape(rows, LANES) + scaled_gmix[...]
     gk[...] = (backward * v_ref[...].astype(F32)).astype(BF16)
@@ -287,8 +289,6 @@
     gq[...] = (c_ref[...].astype(F32) * forward).astype(BF16)
     stores[1].start()
 
-    squared = jnp.sum(sizes[...], axis=0)
-    factor = jnp.minimum(1.0, math.sqrt(entries) / jnp.sqrt(squared + 1e-6))
     for r in range(half):
         fg[r : r + 1, :] = grads[r, 0:1, :] * factor
     stores[4].start()

time: 42.6 us -> 42.5 us (level)
  no operation moved by 1% of the time
where the time goes in v5:
time: 42.5 us; the launch traced here: 42.4 us
  Pallas kernels  41.7 us (98%)
  between operations  0.64 us (2%)
    pallas_call x1, Pallas kernels, per_device(): pl.pallas_call(functools.partial(kernel, C, T), out_shape=(pltpu.VMEM((C,...  40.7 us
    pallas_call x1, Pallas kernels, per_device(): pl.pallas_call(functools.partial(gates, C, entries), out_shape=(slab, sla...  1.04 us

profile of v5, /device:TPU:1, one launch (start us, length us, event | category | flops | bytes accessed | tf_op | source)
XLA Modules:
  0.0 42.4 jit_solution(6548428928386832713)
XLA Ops:
  0.6 40.7 %hyena.1 = (bf16[64,16,128]{2,1,0:T(8,128)(2,1)S(1)}, f32[32,2,128]{2,1,0:T(2,128)S(1)}, f32[8,1,128]{2,1,0:T(1,128)S(1)}, bf16[512,128]{1,0:T(8,128)(2,1)S(1)},...) custom-call(bf16[512,128]{1,0:T(8,128)(2,1)} %q_hbm.1, ...), custom_call_target="tpu_custom_call" | custom-call | tf_op jit(solution)/shard_map/hyena/pallas_call | solution.py:311
  41.3 1.0 %gates.1 = (bf16[512,128]{1,0:T(8,128)(2,1)}, bf16[512,128]{1,0:T(8,128)(2,1)}, bf16[512,128]{1,0:T(8,128)(2,1)}, bf16[512,128]{1,0:T(8,128)(2,1)}, f32[32,128]{1,0:T(8,128)}) custom-call(bf16[64,16,128]{2,1,0:T(8,128)(2,1)S(1)} %get-tuple-element.14.back, f32[32,2,128]{2,1,0:T(2,128)S(1)} %get-tuple-element.15.grads, ...), custom_call_target="tpu_custom_call" | custom-call | tf_op jit(solution)/shard_map/gates/pallas_call | solution.py:347

commit v6 on v5

--- a/solution.py
+++ b/solution.py
@@ -13,6 +13,7 @@
 BF16 = jnp.bfloat16
 LANES = 128
 VMEM_BYTES = 32 * 1024 * 1024
+SPLIT = 1
 UNROLL = 16
 OWN = 8
 
@@ -46,32 +47,34 @@
     core = me % 2
     rows = C * OWN
 
-    def each_peer(start, cores=2):
+    def each_peer(start, cores=2, first=0, stop=Y):
         columns = []
         for j in range(Z):
             plane = lax.rem(z + far(j, Z), Z)
             columns += [2 * Y * plane + 1 - core, 2 * Y * plane + core][2 - cores :]
-        ring(start, columns, False)
-
-    def ring(start, columns, last):
+        ring(start, columns, False, first, stop)
+
+    def ring(start, columns, last, first=0, stop=Y):
         def at(i, _):
             place = 2 * lax.rem(y + far(i, Y), Y)
             for column in columns:
                 start(column + place)
             return 0
 
-        lax.fori_loop(0, Y - 1, at, 0)
+        lax.fori_loop(first, min(stop, Y - 1), at, 0)
+        if stop < Y:
+            return
         for column in columns[:-1]:
             start(column + 2 * y)
         if last is not False:
             pl.when(last)(lambda: start(columns[-1] + 2 * y))
 
     def half_peers(start, late, cores=2):
-        one = lax.rem((z + 1) // 2 + 1 - late, 2)
-        columns = []
-        for plane in (2 * late + one, 2 * late + 1 - one):
-            columns += [2 * Y * plane + 1 - core, 2 * Y * plane + core][2 - cores :]
-        ring(start, columns, z // 2 != late)
+        for plane in (2 * late, 2 * late + 1):
+            ring(start, [2 * Y * plane + 1 - core, 2 * Y * plane + core][2 - cores :], z != plane)
+
+    def plane_peers(start, plane):
+        ring(start, [2 * Y * plane + 1 - core, 2 * Y * plane + core], z != plane)
 
     barrier = pltpu.get_barrier_semaphore()
     each_peer(lambda to: pl.semaphore_signal(barrier, inc=1, device_id=(to, ten), device_id_type=MESH))
@@ -115,8 +118,9 @@
     def send_taps(to):
         send(fsend.at[to // 2], frecv.at[core, pair], 0, (to, ten)).start()
 
+    each_peer(send_main, stop=SPLIT)
     each_peer(send_taps, cores=1)
-    each_peer(send_main)
+    each_peer(send_main, first=SPLIT)
 
     frecv[core, pair] = fsend[pair]
     mrecv[me] = msend[me]
@@ -145,17 +149,6 @@
     tap_swap = send(frecv.at[core], frecv.at[core], 6, (other, ten))
     tap_swap.start()
 
-    tap_swap.wait_recv()
-    def build(n, last):
-        for u in range(UNROLL):
-            d = UNROLL * n + u
-            turned = skew(jnp.broadcast_to(frecv[u % 2, d // 2], (LANES, LANES)))
-            toep[d + 1] = jnp.where(lower, turned, last).astype(BF16)
-            last = turned
-        return last
-
-    lax.fori_loop(0, C // UNROLL, build, jnp.zeros((LANES, LANES), F32))
-
     send(mrecv.at[pl.ds(0, C - 1)], mrecv.at[pl.ds(0, C - 1)], 1, (me, ten)).wait_recv()
     zero = jnp.zeros((OWN, LANES), F32)
     whole = mrecv[...].astype(F32)
@@ -190,6 +183,17 @@
     swap = send(raw, raw_other, 3, (other, ten))
     swap.start()
 
+    tap_swap.wait_recv()
+    def build(n, last):
+        for u in range(UNROLL):
+            d = UNROLL * n + u
+            turned = skew(jnp.broadcast_to(frecv[u % 2, d // 2], (LANES, LANES)))
+            toep[d + 1] = jnp.where(lower, turned, last).astype(BF16)
+            last = turned
+        return last
+
+    lax.fori_loop(0, C // UNROLL, build, jnp.zeros((LANES, LANES), F32))
+
     for j in range(half):
         two = []
         for i in (2 * j, 2 * j + 1):
@@ -235,7 +239,6 @@
 
     half_peers(send_back, 0)
     half_peers(send_grad, 1, cores=1)
-    half_peers(send_back, 1)
     back[me] = bsend[me]
 
     some_grads = grads.at[pl.ds(0, half - 1)]
@@ -245,6 +248,7 @@
     for k in range(1, T):
         send(tsend, sizes.at[ten], 5, (me, lax.rem(ten + k, T))).start()
     sizes[ten] = square
+    half_peers(send_back, 1)
 
     some_back = back.at[pl.ds(0, C - 1)]
     send(some_back, some_back, 2, (me, ten)).wait_recv()

time: 42.5 us -> 41.9 us (0.986)
  Pallas kernels: 41.7 us -> 41.2 us
    pallas_call x1, Pallas kernels: 40.7 us -> 40.1 us  [per_device(): pl.pallas_call(functools.partial(kernel, C, T), out_shape=(pltpu.VMEM((C,...]
where the time goes in v6:
time: 41.9 us; the launch traced here: 41.8 us
  Pallas kernels  41.2 us (98%)
  between operations  0.64 us (2%)
    pallas_call x1, Pallas kernels, per_device(): pl.pallas_call(functools.partial(kernel, C, T), out_shape=(pltpu.VMEM((C,...  40.1 us
    pallas_call x1, Pallas kernels, per_device(): pl.pallas_call(functools.partial(gates, C, entries), out_shape=(slab, sla...  1.04 us

profile of v6, /device:TPU:1, one launch (start us, length us, event | category | flops | bytes accessed | tf_op | source)
XLA Modules:
  0.0 41.8 jit_solution(4243487463185479499)
XLA Ops:
  0.6 40.1 %hyena.1 = (bf16[64,16,128]{2,1,0:T(8,128)(2,1)S(1)}, f32[32,2,128]{2,1,0:T(2,128)S(1)}, f32[8,1,128]{2,1,0:T(1,128)S(1)}, bf16[512,128]{1,0:T(8,128)(2,1)S(1)},...) custom-call(bf16[512,128]{1,0:T(8,128)(2,1)} %q_hbm.1, ...), custom_call_target="tpu_custom_call" | custom-call | tf_op jit(solution)/shard_map/hyena/pallas_call | solution.py:315
  40.8 1.0 %gates.1 = (bf16[512,128]{1,0:T(8,128)(2,1)}, bf16[512,128]{1,0:T(8,128)(2,1)}, bf16[512,128]{1,0:T(8,128)(2,1)}, bf16[512,128]{1,0:T(8,128)(2,1)}, f32[32,128]{1,0:T(8,128)}) custom-call(bf16[64,16,128]{2,1,0:T(8,128)(2,1)S(1)} %get-tuple-element.14.back, f32[32,2,128]{2,1,0:T(2,128)S(1)} %get-tuple-element.15.grads, ...), custom_call_target="tpu_custom_call" | custom-call | tf_op jit(solution)/shard_map/gates/pallas_call | solution.py:351
